TPU v7x, 128 devices: a whole 4x4x4 slice. The times are simulated.
128 devices in a mesh: node: 32 (over z, x, core), local: 4 (over y).
Axes of the slice: x: 4, y: 4, z: 4, core: 2. Of those that a mesh axis runs over, the one named last changes fastest.
Arguments:
- tokens: bfloat16 [2048, 4096], P(('node', 'local')), may hold values from -6 to 6
- expert_ids: int32 [2048, 8], P(('node', 'local')), may hold values from 0 to 127, all different within a row; in each aligned block of 16 rows (0 to 15, 16 to 31, ...) at most 2 rows name the same one
- gate_values: float32 [2048, 8], P(('node', 'local')), may hold values from 0.2 to 1
- w_gate: bfloat16 [128, 4096, 1024], P(('node', 'local')), may hold values from -0.09375 to 0.09375
- w_up: bfloat16 [128, 4096, 1024], P(('node', 'local')), may hold values from -0.09375 to 0.09375
- w_down: bfloat16 [128, 1024, 4096], P(('node', 'local')), may hold values from -0.1875 to 0.1875
Outputs:
- combined: bfloat16 [2048, 4096], P(('node', 'local'))
Inputs may be any that keep to these rules, and one draw needn't show every extreme that they name: `expert_ids`: each row names 8 different experts. Within the 16 rows of one device no expert is named more than 2 times, and in some device one expert is named exactly 2 times.
All inputs are finite; a program needn't handle non-finite values.
Results may differ from a plain program's by a relative error of at most 0.0057.
Values may be sent and summed in bfloat16 or wider, within the bound.
No kernel may reach another device: no remote copies, remote signals or barrier semaphores. Data moves between devices by JAX's collectives and lax.ppermute only.
A program may use at most 128 MiB of HBM per device.

v0:
```python
import jax
import jax.numpy as jnp
from jax import lax
from jax.sharding import PartitionSpec as P


def expert_rows(piece, w_gate, w_up, w_down):
    piece_shape = piece.shape
    flat_rows = piece.reshape(-1, piece_shape[-1])
    gate_part = jnp.dot(flat_rows, w_gate[0], preferred_element_type=jnp.float32)
    up_part = jnp.dot(flat_rows, w_up[0], preferred_element_type=jnp.float32)
    hidden = (jax.nn.silu(gate_part) * up_part).astype(jnp.bfloat16)
    output = jnp.dot(hidden, w_down[0], preferred_element_type=jnp.float32).astype(jnp.bfloat16)
    return output.reshape(piece_shape)


def on_device(tokens, expert_ids, gate_values, w_gate, w_up, w_down):
    node_count = lax.axis_size("node")
    local_count = lax.axis_size("local")
    experts = node_count * local_count
    tok_rows, features = tokens.shape
    top_count = expert_ids.shape[1]
    capacity = max(2, 2 * tok_rows * top_count // experts)
    flat_ids = expert_ids.reshape(-1)
    labels = jnp.arange(experts, dtype=jnp.int32)
    onehot = (flat_ids[:, None] == labels[None, :]).astype(jnp.int32)
    before = jnp.cumsum(onehot, axis=0) - onehot
    slot_index = jnp.sum(before * onehot, axis=1)
    position = flat_ids * capacity + slot_index
    slot_labels = jnp.arange(experts * capacity, dtype=jnp.int32)
    placed = (position[:, None] == slot_labels[None, :]).astype(jnp.float32)
    placed = placed.reshape(tok_rows, top_count, experts * capacity)
    select = jnp.sum(placed, axis=1).astype(jnp.bfloat16)
    outgoing = lax.dot_general(
        select, tokens, (((0,), (0,)), ((), ())), preferred_element_type=jnp.float32
    ).astype(jnp.bfloat16)
    outgoing = outgoing.reshape(experts, capacity, features)
    finished = expert_rows(
        lax.all_to_all(outgoing, ("node", "local"), split_axis=0, concat_axis=0, tiled=True),
        w_gate,
        w_up,
        w_down,
    )
    returned = lax.all_to_all(finished, ("node", "local"), split_axis=0, concat_axis=0, tiled=True)
    weights = jnp.sum(placed * gate_values[:, :, None], axis=1)
    combined = jnp.dot(
        weights,
        returned.reshape(-1, features),
        preferred_element_type=jnp.float32,
        precision=lax.Precision.HIGHEST,
    )
    return combined.astype(jnp.bfloat16)


def solution(mesh):
    in_specs = (
        P(("node", "local"), None),
        P(("node", "local"), None),
        P(("node", "local"), None),
        P(("node", "local"), None, None),
        P(("node", "local"), None, None),
        P(("node", "local"), None, None),
    )
    out_specs = P(("node", "local"), None)
    return jax.shard_map(
        on_device, mesh=mesh, in_specs=in_specs, out_specs=out_specs, check_vma=False
    )
```

profile of v0, /device:TPU:1, one launch (start us, length us, event | category | flops | bytes accessed | tf_op | source)
XLA Modules:
  0.0 110.3 jit_solution(11476752785209439394)
XLA Ops:
  0.0 0.0 copy-start
  0.0 0.8 copy.13
  0.8 0.1 eq.29
  0.9 0.8 copy.15
  1.6 0.1 fusion.18
  1.7 0.2 reduce_window_sum.11
  1.9 0.2 select_reduce_fusion.1
  2.1 0.1 reduce_sum.30
  2.2 0.2 convert_reduce_fusion
  2.4 0.0 copy-done
  2.4 0.7 convolution_convert_fusion
  3.1 2.7 %reshape.32 = bf16[128,2,4096]{2,1,0:T(2,128)(2,1)} reshape(bf16[256,4096]{1,0:T(8,128)(2,1)S(1)} %convolution_convert_fusion) | data formatting | bytes 4194304 | tf_op jit(solution)/shard_map/reshape | solution.py:37
  5.8 42.1 %all_to_all.10 = bf16[128,2,4096]{2,1,0:T(2,128)(2,1)S(1)} all-to-all(bf16[128,2,4096]{2,1,0:T(2,128)(2,1)} %reshape.32), channel_id=1, replica_groups=mesh['node'=32,'local'=4] {'node','local'}, dimensions={0} | all-to-all | bytes 4194304 | tf_op jit(solution)/shard_map/all_to_all | solution.py:39
  47.8 2.2 %reshape.33 = bf16[256,4096]{1,0:T(8,128)(2,1)} reshape(bf16[128,2,4096]{2,1,0:T(2,128)(2,1)S(1)} %all_to_all.10) | data formatting | bytes 4194304 | tf_op jit(solution)/shard_map/reshape | solution.py:9
  50.0 0.0 copy-start.1
  50.0 6.5 %fusion.4 = f32[256,1024]{1,0:T(8,128)S(1)} fusion(bf16[256,4096]{1,0:T(8,128)(2,1)} %reshape.33, bf16[1,4096,1024]{2,1,0:T(8,128)(2,1)} %param.9), kind=kOutput, calls=%fused_computation.4 | convolution fusion | flops 2147483648 | bytes 11534336 | tf_op jit(solution)/shard_map/dot_general | solution.py:10
  56.5 0.0 copy-done.1
  56.5 11.7 %fusion.6 = bf16[256,4096]{1,0:T(8,128)(2,1)} fusion(bf16[1,1024,4096]{2,1,0:T(8,128)(2,1)} %param.11, bf16[256,4096]{1,0:T(8,128)(2,1)S(1)} %copy-done.1, bf16[1,4096,1024]{2,1,0:T(8,128)(2,1)} %param.10, f32[256,1024]{1,0:T(8,128)S(1)} %fusion.4), kind=kOutput, calls=%fused_computation.6 | convolution fusion | flops 4297588736 | bytes 22020096 | tf_op jit(solution)/shard_map/dot_general | solution.py:13
  68.3 3.2 %reshape.34 = bf16[128,2,4096]{2,1,0:T(2,128)(2,1)S(1)} reshape(bf16[256,4096]{1,0:T(8,128)(2,1)} %fusion.6) | data formatting | bytes 4194304 | tf_op jit(solution)/shard_map/reshape | solution.py:14
  71.5 34.5 %all_to_all.11 = bf16[128,2,4096]{2,1,0:T(2,128)(2,1)} all-to-all(bf16[128,2,4096]{2,1,0:T(2,128)(2,1)S(1)} %reshape.34), channel_id=1, replica_groups=mesh['node'=32,'local'=4] {'node','local'}, dimensions={0} | all-to-all | bytes 4194304 | tf_op jit(solution)/shard_map/all_to_all | solution.py:44
  105.9 2.7 %reshape.35 = bf16[256,4096]{1,0:T(8,128)(2,1)S(1)} reshape(bf16[128,2,4096]{2,1,0:T(2,128)(2,1)} %all_to_all.11) | data formatting | bytes 4194304 | tf_op jit(solution)/shard_map/reshape | solution.py:48
  108.7 1.6 %convolution_convert_fusion.1 = bf16[16,4096]{1,0:T(8,128)(2,1)} fusion(f32[16,256]{1,0:T(8,128)S(1)} %get-tuple-element.6, bf16[256,4096]{1,0:T(8,128)(2,1)S(1)} %reshape.35), kind=kOutput, calls=%fused_computation.8 | convolution fusion | flops 201392128 | bytes 2244608 | tf_op jit(solution)/shard_map/dot_general | solution.py:46
  (1 shorter events, 0.0 us)
Async XLA Ops:
  0.0 2.4 %copy-start = (bf16[16,4096]{1,0:T(8,128)(2,1)S(1)}, bf16[16,4096]{1,0:T(8,128)(2,1)}, u32[]{:S(2)}) copy-start(bf16[16,4096]{1,0:T(8,128)(2,1)} %param.6) | copy-start | bytes 393220
  50.0 6.5 %copy-start.1 = (bf16[256,4096]{1,0:T(8,128)(2,1)S(1)}, bf16[256,4096]{1,0:T(8,128)(2,1)}, u32[]{:S(2)}) copy-start(bf16[256,4096]{1,0:T(8,128)(2,1)} %reshape.33) | copy-start | bytes 6291460
where the time goes:
time: 111 us; the launch traced here: 110 us
  blocking collectives  76.5 us (69%)
  matrix products  20.5 us (18%)
  local copies, waits for them, and re-layouts  12.5 us (11%)
    all_to_all x1, blocking collectives, on_device(): lax.all_to_all(outgoing, ('node', 'local'), split_axis=0, concat_axis=0,...  42.1 us
    all_to_all x1, blocking collectives, on_device(): lax.all_to_all(finished, ('node', 'local'), split_axis=0, concat_axis=0,...  34.5 us
    dot_general x1, matrix products, expert_rows(): jnp.dot(hidden, w_down[0], preferred_element_type=jnp.float32)  11.7 us
    dot_general x1, matrix products, expert_rows(): jnp.dot(flat_rows, w_gate[0], preferred_element_type=jnp.float32)  6.48 us
    reshape x1, local copies, waits for them, and re-layouts, expert_rows(): return output.reshape(piece_shape)  3.16 us
    reshape x1, local copies, waits for them, and re-layouts, on_device(): returned.reshape(-1, features)  2.74 us
    reshape x1, local copies, waits for them, and re-layouts, on_device(): outgoing = outgoing.reshape(experts, capacity, features)  2.66 us
    reshape x1, local copies, waits for them, and re-layouts, expert_rows(): flat_rows = piece.reshape(-1, piece_shape[-1])  2.22 us

commit v1 on v0

v1 whole, which is shorter than its diff:
```python
import functools

import jax
import jax.numpy as jnp
from jax import lax
from jax.experimental import pallas as pl
from jax.experimental.pallas import tpu as pltpu
from jax.sharding import PartitionSpec as P

CAP = 2
PARTS = 4
ROWS = CAP * PARTS
BF16 = jnp.bfloat16
F32 = jnp.float32


def vmem(count):
    return [pl.BlockSpec(memory_space=pltpu.VMEM)] * count


def routing(ids_t, experts):
    top, toks = ids_t.shape
    shape = (experts * ROWS, PARTS * toks)
    row = lax.broadcasted_iota(jnp.int32, shape, 0)
    col = lax.broadcasted_iota(jnp.int32, shape, 1)
    wide = jnp.concatenate([ids_t] * PARTS, axis=1)
    named = [(row // ROWS) == wide[k : k + 1, :] for k in range(top)]
    member = functools.reduce(jnp.logical_or, named).astype(F32)
    square = (PARTS * toks, PARTS * toks)
    first = lax.broadcasted_iota(jnp.int32, square, 0)
    second = lax.broadcasted_iota(jnp.int32, square, 1)
    earlier = ((first // toks == second // toks) & (first < second)).astype(F32)
    before = jnp.dot(member.astype(BF16), earlier.astype(BF16), preferred_element_type=F32)
    slot = ((row // PARTS) % CAP).astype(F32)
    own = (before == slot) & (row % PARTS == col // toks)
    return named, member, own


def dispatch_kernel(ids_ref, tok_ref, out_ref, tok_parts, select):
    toks = tok_ref.shape[0]
    wide = tok_parts.shape[1]
    experts = out_ref.shape[0] // ROWS
    for part in range(PARTS):
        tok_parts[part * toks : (part + 1) * toks, :] = tok_ref[:, part * wide : (part + 1) * wide]
    _, member, own = routing(ids_ref[...], experts)
    select[...] = jnp.where(own, member, 0.0).astype(BF16)
    step = 256

    @pl.loop(0, out_ref.shape[0] // step)
    def _(i):
        rows = pl.ds(pl.multiple_of(i * step, step), step)
        out_ref[rows, :] = jnp.dot(select[rows, :], tok_parts[...], preferred_element_type=F32).astype(BF16)


def weights_kernel(ids_ref, gates_ref, out_ref):
    lanes = out_ref.shape[1] // 3
    experts = out_ref.shape[0] // ROWS
    named, _, own = routing(ids_ref[...], experts)
    gates = jnp.concatenate([gates_ref[...]] * PARTS, axis=1)
    total = jnp.zeros(own.shape, F32)
    for k, here in enumerate(named):
        total = total + jnp.where(here, gates[k : k + 1, :], 0.0)
    rest = jnp.where(own, total, 0.0)
    for term in range(3):
        piece = rest.astype(BF16)
        out_ref[:, term * lanes : (term + 1) * lanes] = piece
        rest = rest - piece.astype(F32)


def combine_kernel(weights_ref, rows_ref, out_ref):
    toks = out_ref.shape[0]
    wide = rows_ref.shape[1]
    lanes = weights_ref.shape[1] // 3
    terms = lax.dot_general(
        weights_ref[...], rows_ref[...], (((0,), (0,)), ((), ())), preferred_element_type=F32
    )
    total = terms[:lanes] + terms[lanes : 2 * lanes] + terms[2 * lanes :]
    for part in range(PARTS):
        out_ref[:, part * wide : (part + 1) * wide] = total[part * toks : (part + 1) * toks].astype(BF16)


def expert_kernel(rows_ref, gate_hbm, up_hbm, down_hbm, out_ref, gate, up, down, x, hidden, sems):
    wide = rows_ref.shape[1]
    depth, units = gate.shape
    count = x.shape[0]
    chunk = 256
    pieces = 256 // ROWS
    loads = []
    for i in range(units // chunk):
        cols = pl.ds(i * chunk, chunk)
        loads.append(
            (
                pltpu.make_async_copy(gate_hbm.at[:, cols], gate.at[:, cols], sems.at[0, i]),
                pltpu.make_async_copy(up_hbm.at[:, cols], up.at[:, cols], sems.at[1, i]),
            )
        )
    down_loads = []
    for part in range(PARTS):
        cols = pl.ds(part * wide, wide)
        down_loads.append(pltpu.make_async_copy(down_hbm.at[:, cols], down.at[:, cols], sems.at[2, part]))
    for pair in loads:
        pair[0].start()
        pair[1].start()
    for load in down_loads:
        load.start()
    first = lax.broadcasted_iota(jnp.int32, (256, 256), 0)
    second = lax.broadcasted_iota(jnp.int32, (256, 256), 1)
    ungroup = (second == (first % pieces) * ROWS + first // pieces).astype(F32).astype(BF16)
    group = (first == (second % pieces) * ROWS + second // pieces).astype(F32).astype(BF16)
    half = count // CAP
    for b in range(rows_ref.shape[0] // 256):
        spread = jnp.dot(ungroup, rows_ref[b * 256 : (b + 1) * 256, :], preferred_element_type=F32).astype(BF16)
        for r in range(ROWS):
            slot, part = r // PARTS, r % PARTS
            start = slot * half + b * pieces
            x[start : start + pieces, part * wide : (part + 1) * wide] = spread[r * pieces : (r + 1) * pieces]
    for i in range(units // chunk):
        loads[i][0].wait()
        g = jnp.dot(x[...], gate[:, i * chunk : (i + 1) * chunk], preferred_element_type=F32)
        loads[i][1].wait()
        u = jnp.dot(x[...], up[:, i * chunk : (i + 1) * chunk], preferred_element_type=F32)
        hidden[:, i * chunk : (i + 1) * chunk] = (g / (1.0 + jnp.exp(-g)) * u).astype(BF16)
    for part in range(PARTS):
        down_loads[part].wait()
        y = jnp.dot(hidden[...], down[:, part * wide : (part + 1) * wide], preferred_element_type=F32)
        x[:, part * wide : (part + 1) * wide] = y.astype(BF16)
    for b in range(rows_ref.shape[0] // 256):
        parts = []
        for r in range(ROWS):
            slot, part = r // PARTS, r % PARTS
            start = slot * half + b * pieces
            parts.append(x[start : start + pieces, part * wide : (part + 1) * wide])
        out_ref[b * 256 : (b + 1) * 256, :] = jnp.dot(
            group, jnp.concatenate(parts, axis=0), preferred_element_type=F32
        ).astype(BF16)


def on_device(tokens, expert_ids, gate_values, w_gate, w_up, w_down):
    experts = lax.axis_size("node") * lax.axis_size("local")
    toks, features = tokens.shape
    units = w_gate.shape[2]
    wide = features // PARTS
    lanes = PARTS * toks
    piece_rows = experts * ROWS
    ids_t, gates_t = expert_ids.T, gate_values.T
    slots = jax.ShapeDtypeStruct((piece_rows, wide), BF16)

    def exchange(rows):
        moved = lax.all_to_all(
            rows.reshape(experts, ROWS, wide), ("node", "local"), split_axis=0, concat_axis=0, tiled=True
        )
        return moved.reshape(piece_rows, wide)

    outgoing = pl.pallas_call(
        dispatch_kernel,
        out_shape=slots,
        in_specs=vmem(2),
        out_specs=pl.BlockSpec(memory_space=pltpu.VMEM),
        scratch_shapes=[pltpu.VMEM((lanes, wide), BF16), pltpu.VMEM((piece_rows, lanes), BF16)],
        compiler_params=pltpu.CompilerParams(vmem_limit_bytes=16 << 20),
        name="dispatch",
    )(ids_t, tokens)
    weights = pl.pallas_call(
        weights_kernel,
        out_shape=jax.ShapeDtypeStruct((piece_rows, 3 * lanes), BF16),
        in_specs=vmem(2),
        out_specs=pl.BlockSpec(memory_space=pltpu.VMEM),
        compiler_params=pltpu.CompilerParams(vmem_limit_bytes=16 << 20),
        cost_estimate=pl.CostEstimate(flops=10_000_000, bytes_accessed=1_000_000, transcendentals=0),
        name="weights",
    )(ids_t, gates_t)
    finished = pl.pallas_call(
        expert_kernel,
        out_shape=slots,
        in_specs=vmem(1) + [pl.BlockSpec(memory_space=pl.ANY)] * 3,
        out_specs=pl.BlockSpec(memory_space=pltpu.VMEM),
        scratch_shapes=[
            pltpu.VMEM((features, units), BF16),
            pltpu.VMEM((features, units), BF16),
            pltpu.VMEM((units, features), BF16),
            pltpu.VMEM((experts * CAP, features), BF16),
            pltpu.VMEM((experts * CAP, units), BF16),
            pltpu.SemaphoreType.DMA((3, 4)),
        ],
        compiler_params=pltpu.CompilerParams(vmem_limit_bytes=44 << 20),
        name="expert",
    )(exchange(outgoing), w_gate[0], w_up[0], w_down[0])
    return pl.pallas_call(
        combine_kernel,
        out_shape=jax.ShapeDtypeStruct((toks, features), BF16),
        in_specs=vmem(2),
        out_specs=pl.BlockSpec(memory_space=pltpu.VMEM),
        compiler_params=pltpu.CompilerParams(vmem_limit_bytes=16 << 20),
        name="combine",
    )(weights, exchange(finished))


def solution(mesh):
    rows = P(("node", "local"), None)
    block = P(("node", "local"), None, None)
    return jax.shard_map(
        on_device,
        mesh=mesh,
        in_specs=(rows, rows, rows, block, block, block),
        out_specs=rows,
        check_vma=False,
    )
```

time: 111 us -> 98.1 us (0.88)
  blocking collectives: 76.5 us -> 41.9 us
  waiting for transfers between devices: 0 us -> 29.3 us
  Pallas kernels: 0 us -> 21.2 us
  matrix products: 20.5 us -> 0 us
  local copies, waits for them, and re-layouts: 12.5 us -> 1.6 us
  starting transfers between devices: 0 us -> 3.83 us
    all_to_all x2 -> x1, blocking collectives: 76.5 us -> 41.9 us  [exchange(): lax.all_to_all(rows.reshape(experts, ROWS, wide), ('node', 'local'), spli...]
    all_to_all x0 -> x1, waiting for transfers between devices: none -> 29.3 us  [exchange(): lax.all_to_all(rows.reshape(experts, ROWS, wide), ('node', 'local'), spli...]
    pallas_call x0 -> x4, Pallas kernels: none -> 21.2 us  [the longest x1 16.8 us: on_device(): pl.pallas_call(expert_kernel, out_shape=slots, in_specs=vmem(1) + [pl.Blo...]
    dot_general x4 -> x0, matrix products: 20.5 us -> none  [the longest x1 11.7 us: expert_rows(): jnp.dot(hidden, w_down[0], preferred_element_type=jnp.float32)]
    reshape x4 -> x0, local copies, waits for them, and re-layouts: 10.8 us -> none  [the longest x1 3.16 us: expert_rows(): return output.reshape(piece_shape)]
    all_to_all x0 -> x1, starting transfers between devices: none -> 3.83 us  [exchange(): lax.all_to_all(rows.reshape(experts, ROWS, wide), ('node', 'local'), spli...]
  transfers between devices with their start and end apart: 0 -> 1, of which waited for: 0 -> 1; matrix products, arithmetic and copies ran while one was open for 0% -> 0% of each run, Pallas kernels for 0% -> 1%
where the time goes in v1:
time: 98.1 us; the launch traced here: 97.9 us
  blocking collectives  41.9 us (43%)
  waiting for transfers between devices  29.3 us (30%)
  Pallas kernels  21.2 us (22%)
  starting transfers between devices  3.83 us (4%)
  local copies, waits for them, and re-layouts  1.6 us (2%)
    all_to_all x1, blocking collectives, exchange(): lax.all_to_all(rows.reshape(experts, ROWS, wide), ('node', 'local'), spli...  41.9 us
    all_to_all x1, waiting for transfers between devices, exchange(): lax.all_to_all(rows.reshape(experts, ROWS, wide), ('node', 'local'), spli...  29.3 us
    pallas_call x1, Pallas kernels, on_device(): pl.pallas_call(expert_kernel, out_shape=slots, in_specs=vmem(1) + [pl.Blo...  16.8 us
    all_to_all x1, starting transfers between devices, exchange(): lax.all_to_all(rows.reshape(experts, ROWS, wide), ('node', 'local'), spli...  3.83 us
  transfers between devices with their start and end apart: 1, of which 1 were waited for; matrix products, arithmetic and copies ran while one was open for 0% of the time, Pallas kernels for 1%

profile of v1, /device:TPU:1, one launch (start us, length us, event | category | flops | bytes accessed | tf_op | source)
XLA Modules:
  0.0 97.9 jit_solution(7801543460344187635)
XLA Ops:
  0.0 0.0 copy-start
  0.0 0.9 copy-done
  0.9 0.0 copy-start.1
  0.9 0.7 copy-done.1
  1.6 1.8 %dispatch.1 = bf16[1024,1024]{1,0:T(8,128)(2,1)S(1)} custom-call(s32[8,16]{1,0:T(8,128)S(1)} %bitcast.12, bf16[16,4096]{1,0:T(8,128)(2,1)S(1)} %copy-done), custom_call_target="tpu_custom_call" | custom-call | tf_op jit(solution)/shard_map/dispatch/pallas_call | solution.py:154
  3.4 41.9 %all_to_all.10 = bf16[128,8,1024]{2,1,0:T(8,128)(2,1)S(1)} all-to-all(bf16[128,8,1024]{2,1,0:T(8,128)(2,1)S(1)} %bitcast.11), channel_id=1, replica_groups=mesh['node'=32,'local'=4] {'node','local'}, dimensions={0} | all-to-all | bytes 4194304 | tf_op jit(solution)/shard_map/all_to_all | solution.py:149
  45.3 16.8 %expert.1 = bf16[1024,1024]{1,0:T(8,128)(2,1)} custom-call(bf16[1024,1024]{1,0:T(8,128)(2,1)S(1)} %bitcast.9, bf16[4096,1024]{1,0:T(8,128)(2,1)} %bitcast.15, bf16[4096,1024]{1,0:T(8,128)(2,1)} %bitcast.16, bf16[1024,4096]{1,0:T(8,128)(2,1)} %bitcast.17), custom_call_target="tpu_custom_call" | custom-call | tf_op jit(solution)/shard_map/expert/pallas_call | solution.py:172
  62.1 0.0 copy-start.2
  62.1 0.0 copy-start.3
  62.1 3.8 %all-to-all-start.1 = ((bf16[128,8,1024]{2,1,0:T(8,128)(2,1)}), bf16[128,8,1024]{2,1,0:T(8,128)(2,1)S(1)}, u32[]{:S(2)}, u32[]{:S(2)}) async-start(bf16[128,8,1024]{2,1,0:T(8,128)(2,1)} %bitcast.7), calls=%async_computation.1 | async-start | bytes 4194304 | tf_op jit(solution)/shard_map/all_to_all | solution.py:149
  66.0 0.0 copy-done.2
  66.0 0.0 copy-done.3
  66.0 1.3 %weights.1.weights_ref = bf16[1024,192]{1,0:T(8,128)(2,1)S(1)} custom-call(s32[8,16]{1,0:T(8,128)S(1)} %bitcast.13, f32[8,16]{1,0:T(8,128)S(1)} %bitcast.14), custom_call_target="tpu_custom_call" | custom-call | flops 10000000 | bytes 1000000 | tf_op jit(solution)/shard_map/weights/pallas_call | solution.py:163
  67.3 29.3 %all-to-all-done.1 = bf16[128,8,1024]{2,1,0:T(8,128)(2,1)S(1)} async-done(((bf16[128,8,1024]{2,1,0:T(8,128)(2,1)}), bf16[128,8,1024]{2,1,0:T(8,128)(2,1)S(1)}, u32[]{:S(2)}, u32[]{:S(2)}) %all-to-all-start.1) | async-done | bytes 2097184 | tf_op jit(solution)/shard_map/all_to_all | solution.py:149
  96.6 1.3 %combine.1 = bf16[16,4096]{1,0:T(8,128)(2,1)} custom-call(bf16[1024,192]{1,0:T(8,128)(2,1)S(1)} %weights.1.weights_ref, bf16[1024,1024]{1,0:T(8,128)(2,1)S(1)} %bitcast.10), custom_call_target="tpu_custom_call" | custom-call | tf_op jit(solution)/shard_map/combine/pallas_call | solution.py:188
Async XLA Ops:
  0.0 0.9 copy-start
  0.9 0.7 copy-start.1
  62.1 3.9 %copy-start.2 = (s32[16,8]{0,1:T(8,128)S(1)}, s32[16,8]{0,1:T(8,128)}, u32[]{:S(2)}) copy-start(s32[16,8]{0,1:T(8,128)} %param.7) | copy-start | bytes 1540
  62.1 3.9 %copy-start.3 = (f32[16,8]{0,1:T(8,128)S(1)}, f32[16,8]{0,1:T(8,128)}, u32[]{:S(2)}) copy-start(f32[16,8]{0,1:T(8,128)} %param.8) | copy-start | bytes 1540
  62.1 34.5 %all-to-all-start.1 = ((bf16[128,8,1024]{2,1,0:T(8,128)(2,1)}), bf16[128,8,1024]{2,1,0:T(8,128)(2,1)S(1)}, u32[]{:S(2)}, u32[]{:S(2)}) async-start(bf16[128,8,1024]{2,1,0:T(8,128)(2,1)} %bitcast.7), calls=%async_computation.1 | async-start | bytes 4194304 | tf_op jit(solution)/shard_map/all_to_all | solution.py:149

commit v2 on v1

--- a/solution.py
+++ b/solution.py
@@ -79,30 +79,12 @@
         out_ref[:, part * wide : (part + 1) * wide] = total[part * toks : (part + 1) * toks].astype(BF16)
 
 
-def expert_kernel(rows_ref, gate_hbm, up_hbm, down_hbm, out_ref, gate, up, down, x, hidden, sems):
+def expert_kernel(rows_ref, gate_ref, up_ref, down_ref, out_ref, x, hidden):
     wide = rows_ref.shape[1]
-    depth, units = gate.shape
+    units = gate_ref.shape[1]
     count = x.shape[0]
     chunk = 256
     pieces = 256 // ROWS
-    loads = []
-    for i in range(units // chunk):
-        cols = pl.ds(i * chunk, chunk)
-        loads.append(
-            (
-                pltpu.make_async_copy(gate_hbm.at[:, cols], gate.at[:, cols], sems.at[0, i]),
-                pltpu.make_async_copy(up_hbm.at[:, cols], up.at[:, cols], sems.at[1, i]),
-            )
-        )
-    down_loads = []
-    for part in range(PARTS):
-        cols = pl.ds(part * wide, wide)
-        down_loads.append(pltpu.make_async_copy(down_hbm.at[:, cols], down.at[:, cols], sems.at[2, part]))
-    for pair in loads:
-        pair[0].start()
-        pair[1].start()
-    for load in down_loads:
-        load.start()
     first = lax.broadcasted_iota(jnp.int32, (256, 256), 0)
     second = lax.broadcasted_iota(jnp.int32, (256, 256), 1)
     ungroup = (second == (first % pieces) * ROWS + first // pieces).astype(F32).astype(BF16)
@@ -115,15 +97,13 @@
             start = slot * half + b * pieces
             x[start : start + pieces, part * wide : (part + 1) * wide] = spread[r * pieces : (r + 1) * pieces]
     for i in range(units // chunk):
-        loads[i][0].wait()
-        g = jnp.dot(x[...], gate[:, i * chunk : (i + 1) * chunk], preferred_element_type=F32)
-        loads[i][1].wait()
-        u = jnp.dot(x[...], up[:, i * chunk : (i + 1) * chunk], preferred_element_type=F32)
-        hidden[:, i * chunk : (i + 1) * chunk] = (g / (1.0 + jnp.exp(-g)) * u).astype(BF16)
+        cols = slice(i * chunk, (i + 1) * chunk)
+        g = jnp.dot(x[...], gate_ref[:, cols], preferred_element_type=F32)
+        u = jnp.dot(x[...], up_ref[:, cols], preferred_element_type=F32)
+        hidden[:, cols] = (g / (1.0 + jnp.exp(-g)) * u).astype(BF16)
     for part in range(PARTS):
-        down_loads[part].wait()
-        y = jnp.dot(hidden[...], down[:, part * wide : (part + 1) * wide], preferred_element_type=F32)
-        x[:, part * wide : (part + 1) * wide] = y.astype(BF16)
+        cols = slice(part * wide, (part + 1) * wide)
+        x[:, cols] = jnp.dot(hidden[...], down_ref[:, cols], preferred_element_type=F32).astype(BF16)
     for b in range(rows_ref.shape[0] // 256):
         parts = []
         for r in range(ROWS):
@@ -158,6 +138,7 @@
         out_specs=pl.BlockSpec(memory_space=pltpu.VMEM),
         scratch_shapes=[pltpu.VMEM((lanes, wide), BF16), pltpu.VMEM((piece_rows, lanes), BF16)],
         compiler_params=pltpu.CompilerParams(vmem_limit_bytes=16 << 20),
+        cost_estimate=pl.CostEstimate(flops=20_000_000_000, bytes_accessed=100_000_000, transcendentals=0),
         name="dispatch",
     )(ids_t, tokens)
     weights = pl.pallas_call(
@@ -172,17 +153,14 @@
     finished = pl.pallas_call(
         expert_kernel,
         out_shape=slots,
-        in_specs=vmem(1) + [pl.BlockSpec(memory_space=pl.ANY)] * 3,
+        in_specs=vmem(4),
         out_specs=pl.BlockSpec(memory_space=pltpu.VMEM),
         scratch_shapes=[
-            pltpu.VMEM((features, units), BF16),
-            pltpu.VMEM((features, units), BF16),
-            pltpu.VMEM((units, features), BF16),
             pltpu.VMEM((experts * CAP, features), BF16),
             pltpu.VMEM((experts * CAP, units), BF16),
-            pltpu.SemaphoreType.DMA((3, 4)),
         ],
-        compiler_params=pltpu.CompilerParams(vmem_limit_bytes=44 << 20),
+        compiler_params=pltpu.CompilerParams(vmem_limit_bytes=16 << 20),
+        cost_estimate=pl.CostEstimate(flops=6_500_000_000, bytes_accessed=30_000_000, transcendentals=0),
         name="expert",
     )(exchange(outgoing), w_gate[0], w_up[0], w_down[0])
     return pl.pallas_call(

time: 98.1 us -> 91.3 us (0.931)
  Pallas kernels: 21.2 us -> 13.7 us
    pallas_call x1, Pallas kernels: 16.8 us -> 9.29 us  [on_device(): pl.pallas_call(expert_kernel, out_shape=slots, in_specs=vmem(4), out_spec...]
    unnamed x8 -> x20, local copies, waits for them, and re-layouts: 1.6 us -> 2.19 us
where the time goes in v2:
time: 91.3 us; the launch traced here: 91.1 us
  blocking collectives  41.9 us (46%)
  waiting for transfers between devices  29.4 us (32%)
  Pallas kernels  13.7 us (15%)
  starting transfers between devices  3.88 us (4%)
  local copies, waits for them, and re-layouts  2.19 us (2%)
    all_to_all x1, blocking collectives, exchange(): lax.all_to_all(rows.reshape(experts, ROWS, wide), ('node', 'local'), spli...  41.9 us
    all_to_all x1, waiting for transfers between devices, exchange(): lax.all_to_all(rows.reshape(experts, ROWS, wide), ('node', 'local'), spli...  29.4 us
    pallas_call x1, Pallas kernels, on_device(): pl.pallas_call(expert_kernel, out_shape=slots, in_specs=vmem(4), out_spec...  9.29 us
    all_to_all x1, starting transfers between devices, exchange(): lax.all_to_all(rows.reshape(experts, ROWS, wide), ('node', 'local'), spli...  3.88 us
    unnamed x20, local copies, waits for them, and re-layouts  2.19 us
  transfers between devices with their start and end apart: 1, of which 1 were waited for; matrix products, arithmetic and copies ran while one was open for 0% of the time, Pallas kernels for 1%

profile of v2, /device:TPU:1, one launch (start us, length us, event | category | flops | bytes accessed | tf_op | source)
XLA Modules:
  0.0 91.1 jit_solution(407595509845673753)
XLA Ops:
  0.0 0.0 slice-start
  0.0 0.0 slice-start.2
  0.0 0.0 copy-start
  0.0 0.8 copy-done
  0.8 0.0 copy-start.3
  0.9 1.3 %copy-done.3 = bf16[16,4096]{1,0:T(8,128)(2,1)S(1)} copy-done((bf16[16,4096]{1,0:T(8,128)(2,1)S(1)}, bf16[16,4096]{1,0:T(8,128)(2,1)}, u32[]{:S(2)}) %copy-start.3) | copy-done | bytes 131096
  2.2 0.0 slice-start.1
  2.2 0.0 slice-start.3
  2.2 0.0 slice-start.5
  2.2 1.8 %dispatch.1 = bf16[1024,1024]{1,0:T(8,128)(2,1)S(1)} custom-call(s32[8,16]{1,0:T(8,128)S(1)} %bitcast.21, bf16[16,4096]{1,0:T(8,128)(2,1)S(1)} %copy-done.3), custom_call_target="tpu_custom_call" | custom-call | flops 20000000000 | bytes 100000000 | tf_op jit(solution)/shard_map/dispatch/pallas_call | solution.py:134
  4.0 41.9 %all_to_all.10 = bf16[128,8,1024]{2,1,0:T(8,128)(2,1)S(1)} all-to-all(bf16[128,8,1024]{2,1,0:T(8,128)(2,1)S(1)} %bitcast.20), channel_id=1, replica_groups=mesh['node'=32,'local'=4] {'node','local'}, dimensions={0} | all-to-all | bytes 4194304 | tf_op jit(solution)/shard_map/all_to_all | solution.py:129
  45.8 0.0 slice-done
  45.8 0.0 slice-done.2
  45.8 0.0 slice-done.4
  45.9 0.0 slice-done.1
  45.9 0.0 slice-done.3
  45.9 0.0 slice-done.5
  45.9 9.3 %expert.1 = bf16[1024,1024]{1,0:T(8,128)(2,1)} custom-call(bf16[1024,1024]{1,0:T(8,128)(2,1)S(1)} %bitcast.9, bf16[4096,1024]{1,0:T(8,128)(2,1)S(1)} %bitcast.12, bf16[4096,1024]{1,0:T(8,128)(2,1)S(1)} %bitcast.15, bf16[1024,4096]{1,0:T(8,128)(2,1)S(1)} %bitcast.18), custom_call_target="tpu_custom_call" | custom-call | flops 6499999744 | bytes 30000000 | tf_op jit(solution)/shard_map/expert/pallas_call | solution.py:153
  55.2 3.9 %all-to-all-start.1 = ((bf16[128,8,1024]{2,1,0:T(8,128)(2,1)}), bf16[128,8,1024]{2,1,0:T(8,128)(2,1)S(1)}, u32[]{:S(2)}, u32[]{:S(2)}) async-start(bf16[128,8,1024]{2,1,0:T(8,128)(2,1)} %bitcast.7), calls=%async_computation.1 | async-start | bytes 4194304 | tf_op jit(solution)/shard_map/all_to_all | solution.py:129
  59.1 0.0 copy-done.1
  59.1 0.0 copy-done.2
  59.1 1.3 %weights.1.weights_ref = bf16[1024,192]{1,0:T(8,128)(2,1)S(1)} custom-call(s32[8,16]{1,0:T(8,128)S(1)} %bitcast.22, f32[8,16]{1,0:T(8,128)S(1)} %bitcast.23), custom_call_target="tpu_custom_call" | custom-call | flops 10000000 | bytes 1000000 | tf_op jit(solution)/shard_map/weights/pallas_call | solution.py:144
  60.4 29.4 %all-to-all-done.1 = bf16[128,8,1024]{2,1,0:T(8,128)(2,1)S(1)} async-done(((bf16[128,8,1024]{2,1,0:T(8,128)(2,1)}), bf16[128,8,1024]{2,1,0:T(8,128)(2,1)S(1)}, u32[]{:S(2)}, u32[]{:S(2)}) %all-to-all-start.1) | async-done | bytes 2097184 | tf_op jit(solution)/shard_map/all_to_all | solution.py:129
  89.8 1.3 %combine.1 = bf16[16,4096]{1,0:T(8,128)(2,1)} custom-call(bf16[1024,192]{1,0:T(8,128)(2,1)S(1)} %weights.1.weights_ref, bf16[1024,1024]{1,0:T(8,128)(2,1)S(1)} %bitcast.19), custom_call_target="tpu_custom_call" | custom-call | tf_op jit(solution)/shard_map/combine/pallas_call | solution.py:166
  (6 shorter events, 0.0 us)
Async XLA Ops:
  0.0 45.8 %slice-start = ((s8[8388608]{0:T(1024)(128)(4,1)}), s8[4194304]{0:T(1024)(128)(4,1)S(1)}, s32[]{:S(2)}) async-start(s8[8388608]{0:T(1024)(128)(4,1)} %bitcast.10), calls=%async_computation.2 | async-start | bytes 8388608
  0.0 45.8 %slice-start.2 = ((s8[8388608]{0:T(1024)(128)(4,1)}), s8[4194304]{0:T(1024)(128)(4,1)S(1)}, s32[]{:S(2)}) async-start(s8[8388608]{0:T(1024)(128)(4,1)} %bitcast.13), calls=%async_computation.4 | async-start | bytes 8388608
  0.0 45.8 %slice-start.4 = ((s8[8388608]{0:T(1024)(128)(4,1)}), s8[4194304]{0:T(1024)(128)(4,1)S(1)}, s32[]{:S(2)}) async-start(s8[8388608]{0:T(1024)(128)(4,1)} %bitcast.16), calls=%async_computation.6 | async-start | bytes 8388608
  0.0 0.8 copy-start
  0.8 1.3 %copy-start.3 = (bf16[16,4096]{1,0:T(8,128)(2,1)S(1)}, bf16[16,4096]{1,0:T(8,128)(2,1)}, u32[]{:S(2)}) copy-start(bf16[16,4096]{1,0:T(8,128)(2,1)} %tok_ref.1) | copy-start | bytes 393220
  2.2 43.7 %slice-start.1 = ((s8[8388608]{0:T(1024)(128)(4,1)}), s8[4194304]{0:T(1024)(128)(4,1)S(1)}, s32[]{:S(2)}) async-start(s8[8388608]{0:T(1024)(128)(4,1)} %bitcast.10), calls=%async_computation.3 | async-start | bytes 8388608
  2.2 43.7 %slice-start.3 = ((s8[8388608]{0:T(1024)(128)(4,1)}), s8[4194304]{0:T(1024)(128)(4,1)S(1)}, s32[]{:S(2)}) async-start(s8[8388608]{0:T(1024)(128)(4,1)} %bitcast.13), calls=%async_computation.5 | async-start | bytes 8388608
  2.2 43.7 %slice-start.5 = ((s8[8388608]{0:T(1024)(128)(4,1)}), s8[4194304]{0:T(1024)(128)(4,1)S(1)}, s32[]{:S(2)}) async-start(s8[8388608]{0:T(1024)(128)(4,1)} %bitcast.16), calls=%async_computation.7 | async-start | bytes 8388608
  55.2 3.9 %copy-start.1 = (s32[16,8]{0,1:T(8,128)S(1)}, s32[16,8]{0,1:T(8,128)}, u32[]{:S(2)}) copy-start(s32[16,8]{0,1:T(8,128)} %param.7) | copy-start | bytes 1540
  55.2 3.9 %copy-start.2 = (f32[16,8]{0,1:T(8,128)S(1)}, f32[16,8]{0,1:T(8,128)}, u32[]{:S(2)}) copy-start(f32[16,8]{0,1:T(8,128)} %param.8) | copy-start | bytes 1540
  55.2 34.6 %all-to-all-start.1 = ((bf16[128,8,1024]{2,1,0:T(8,128)(2,1)}), bf16[128,8,1024]{2,1,0:T(8,128)(2,1)S(1)}, u32[]{:S(2)}, u32[]{:S(2)}) async-start(bf16[128,8,1024]{2,1,0:T(8,128)(2,1)} %bitcast.7), calls=%async_computation.1 | async-start | bytes 4194304 | tf_op jit(solution)/shard_map/all_to_all | solution.py:129

commit v3 on v2

v3 whole, which is shorter than its diff:
```python
import functools

import jax
import jax.numpy as jnp
from jax import lax
from jax.experimental import pallas as pl
from jax.experimental.pallas import tpu as pltpu
from jax.sharding import PartitionSpec as P

CAP = 2
PARTS = 4
ROWS = CAP * PARTS
BF16 = jnp.bfloat16
F32 = jnp.float32


def vmem(count):
    return [pl.BlockSpec(memory_space=pltpu.VMEM)] * count


def lane_columns(wide_t):
    top, toks = wide_t.shape
    return jnp.concatenate([wide_t] * (128 // toks), axis=1).T[: PARTS * toks]


def routing(ids_t, values_t, experts):
    top, toks = ids_t.shape
    shape = (PARTS * toks, experts * ROWS)
    lane = lax.broadcasted_iota(jnp.int32, shape, 0)
    row = lax.broadcasted_iota(jnp.int32, shape, 1)
    ids = lane_columns(ids_t)
    expert = row // ROWS
    named = [expert == ids[:, k : k + 1] for k in range(top)]
    member = functools.reduce(jnp.logical_or, named).astype(F32)
    square = (PARTS * toks, PARTS * toks)
    later = lax.broadcasted_iota(jnp.int32, square, 0)
    sooner = lax.broadcasted_iota(jnp.int32, square, 1)
    earlier = ((later // toks == sooner // toks) & (sooner < later)).astype(F32).astype(BF16)
    before = jnp.dot(earlier, member.astype(BF16), preferred_element_type=F32)
    slot = ((row // PARTS) % CAP).astype(F32)
    own = (before == slot) & (row % PARTS == lane // toks)
    if values_t is not None:
        values = lane_columns(values_t)
        member = jnp.zeros(shape, F32)
        for k, here in enumerate(named):
            member = jnp.where(here, values[:, k : k + 1], member)
    return jnp.where(own, member, 0.0)


def dispatch_kernel(ids_hbm, tok_hbm, out_ref, ids_ref, tok_parts, sems):
    toks = tok_hbm.shape[0]
    wide = tok_parts.shape[1]
    experts = out_ref.shape[0] // ROWS
    ids_load = pltpu.make_async_copy(ids_hbm, ids_ref, sems.at[PARTS])
    ids_load.start()
    loads = []
    for part in range(PARTS):
        source = tok_hbm.at[:, pl.ds(part * wide, wide)]
        loads.append(pltpu.make_async_copy(source, tok_parts.at[pl.ds(part * toks, toks), :], sems.at[part]))
        loads[-1].start()
    ids_load.wait()
    select = routing(ids_ref[...], None, experts).astype(BF16)
    for load in loads:
        load.wait()
    out_ref[...] = lax.dot_general(
        select, tok_parts[...], (((0,), (0,)), ((), ())), preferred_element_type=F32
    ).astype(BF16)


def combine_weights(ids_t, gates_t, out_ref):
    lanes = out_ref.shape[0] // 3
    rest = routing(ids_t, gates_t, out_ref.shape[1] // ROWS)
    for term in range(3):
        piece = rest.astype(BF16)
        out_ref[term * lanes : (term + 1) * lanes, :] = piece
        rest = rest - piece.astype(F32)


def combine_kernel(weights_ref, rows_ref, out_ref):
    toks = out_ref.shape[0]
    wide = rows_ref.shape[1]
    lanes = weights_ref.shape[0] // 3
    terms = jnp.dot(weights_ref[...], rows_ref[...], preferred_element_type=F32)
    total = terms[:lanes] + terms[lanes : 2 * lanes] + terms[2 * lanes :]
    for part in range(PARTS):
        out_ref[:, part * wide : (part + 1) * wide] = total[part * toks : (part + 1) * toks].astype(BF16)


def expert_kernel(ids_ref, gates_ref, rows_ref, gate_ref, up_ref, down_ref, out_ref, weights_ref, x, hidden):
    wide = rows_ref.shape[1]
    units = gate_ref.shape[1]
    count = x.shape[0]
    chunk = 256
    pieces = 256 // ROWS
    first = lax.broadcasted_iota(jnp.int32, (256, 256), 0)
    second = lax.broadcasted_iota(jnp.int32, (256, 256), 1)
    ungroup = (second == (first % pieces) * ROWS + first // pieces).astype(F32).astype(BF16)
    group = (first == (second % pieces) * ROWS + second // pieces).astype(F32).astype(BF16)
    half = count // CAP
    for b in range(rows_ref.shape[0] // 256):
        spread = jnp.dot(ungroup, rows_ref[b * 256 : (b + 1) * 256, :], preferred_element_type=F32).astype(BF16)
        for r in range(ROWS):
            slot, part = r // PARTS, r % PARTS
            start = slot * half + b * pieces
            x[start : start + pieces, part * wide : (part + 1) * wide] = spread[r * pieces : (r + 1) * pieces]
    for i in range(units // chunk):
        cols = slice(i * chunk, (i + 1) * chunk)
        g = jnp.dot(x[...], gate_ref[:, cols], preferred_element_type=F32)
        u = jnp.dot(x[...], up_ref[:, cols], preferred_element_type=F32)
        hidden[:, cols] = (g / (1.0 + jnp.exp(-g)) * u).astype(BF16)
        if i == 0:
            combine_weights(ids_ref[...], gates_ref[...], weights_ref)
    for part in range(PARTS):
        cols = slice(part * wide, (part + 1) * wide)
        x[:, cols] = jnp.dot(hidden[...], down_ref[:, cols], preferred_element_type=F32).astype(BF16)
    for b in range(rows_ref.shape[0] // 256):
        parts = []
        for r in range(ROWS):
            slot, part = r // PARTS, r % PARTS
            start = slot * half + b * pieces
            parts.append(x[start : start + pieces, part * wide : (part + 1) * wide])
        out_ref[b * 256 : (b + 1) * 256, :] = jnp.dot(
            group, jnp.concatenate(parts, axis=0), preferred_element_type=F32
        ).astype(BF16)


def on_device(tokens, expert_ids, gate_values, w_gate, w_up, w_down):
    experts = lax.axis_size("node") * lax.axis_size("local")
    toks, features = tokens.shape
    units = w_gate.shape[2]
    wide = features // PARTS
    lanes = PARTS * toks
    piece_rows = experts * ROWS
    ids_t, gates_t = expert_ids.T, gate_values.T
    slots = jax.ShapeDtypeStruct((piece_rows, wide), BF16)

    def exchange(rows):
        moved = lax.all_to_all(
            rows.reshape(experts, ROWS, wide), ("node", "local"), split_axis=0, concat_axis=0, tiled=True
        )
        return moved.reshape(piece_rows, wide)

    outgoing = pl.pallas_call(
        dispatch_kernel,
        out_shape=slots,
        in_specs=[pl.BlockSpec(memory_space=pltpu.HBM)] * 2,
        out_specs=pl.BlockSpec(memory_space=pltpu.VMEM),
        scratch_shapes=[
            pltpu.VMEM(ids_t.shape, jnp.int32),
            pltpu.VMEM((lanes, wide), BF16),
            pltpu.SemaphoreType.DMA((PARTS + 1,)),
        ],
        compiler_params=pltpu.CompilerParams(vmem_limit_bytes=16 << 20),
        cost_estimate=pl.CostEstimate(flops=20_000_000_000, bytes_accessed=100_000_000, transcendentals=0),
        name="dispatch",
    )(pltpu.with_memory_space_constraint(ids_t, pltpu.HBM), pltpu.with_memory_space_constraint(tokens, pltpu.HBM))
    finished, weights = pl.pallas_call(
        expert_kernel,
        out_shape=[slots, jax.ShapeDtypeStruct((3 * lanes, piece_rows), BF16)],
        in_specs=vmem(6),
        out_specs=vmem(2),
        scratch_shapes=[
            pltpu.VMEM((experts * CAP, features), BF16),
            pltpu.VMEM((experts * CAP, units), BF16),
        ],
        compiler_params=pltpu.CompilerParams(vmem_limit_bytes=16 << 20),
        cost_estimate=pl.CostEstimate(flops=6_500_000_000, bytes_accessed=30_000_000, transcendentals=0),
        name="expert",
    )(ids_t, gates_t, exchange(outgoing), w_gate[0], w_up[0], w_down[0])
    return pl.pallas_call(
        combine_kernel,
        out_shape=jax.ShapeDtypeStruct((toks, features), BF16),
        in_specs=vmem(2),
        out_specs=pl.BlockSpec(memory_space=pltpu.VMEM),
        compiler_params=pltpu.CompilerParams(vmem_limit_bytes=16 << 20),
        name="combine",
    )(weights, exchange(finished))


def solution(mesh):
    rows = P(("node", "local"), None)
    block = P(("node", "local"), None, None)
    return jax.shard_map(
        on_device,
        mesh=mesh,
        in_specs=(rows, rows, rows, block, block, block),
        out_specs=rows,
        check_vma=False,
    )
```

time: 91.3 us -> 88.1 us (0.965)
  blocking collectives: 41.9 us -> 76.1 us
  waiting for transfers between devices: 29.4 us -> 0 us
  starting transfers between devices: 3.88 us -> 0 us
  local copies, waits for them, and re-layouts: 2.19 us -> 0.04 us
  Pallas kernels: 13.7 us -> 11.8 us
    all_to_all x1 -> x2, blocking collectives: 41.9 us -> 76.1 us  [exchange(): lax.all_to_all(rows.reshape(experts, ROWS, wide), ('node', 'local'), spli...]
    all_to_all x1 -> x0, waiting for transfers between devices: 29.4 us -> none  [exchange(): lax.all_to_all(rows.reshape(experts, ROWS, wide), ('node', 'local'), spli...]
    all_to_all x1 -> x0, starting transfers between devices: 3.88 us -> none  [exchange(): lax.all_to_all(rows.reshape(experts, ROWS, wide), ('node', 'local'), spli...]
    unnamed x20 -> x16, local copies, waits for them, and re-layouts: 2.19 us -> 0.04 us
    pallas_call x3 -> x2, Pallas kernels: 12.4 us -> 10.5 us  [the longest x1 8.3 us: on_device(): pl.pallas_call(expert_kernel, out_shape=[slots, jax.ShapeDtypeStruct((3 *...]
  transfers between devices with their start and end apart: 1 -> 0, of which waited for: 1 -> 0; matrix products, arithmetic and copies ran while one was open for 0% -> 0% of each run, Pallas kernels for 1% -> 0%
where the time goes in v3:
time: 88.1 us; the launch traced here: 88 us
  blocking collectives  76.1 us (86%)
  Pallas kernels  11.8 us (13%)
    all_to_all x2, blocking collectives, exchange(): lax.all_to_all(rows.reshape(experts, ROWS, wide), ('node', 'local'), spli...  76.1 us
    pallas_call x1, Pallas kernels, on_device(): pl.pallas_call(expert_kernel, out_shape=[slots, jax.ShapeDtypeStruct((3 *...  8.3 us
    pallas_call x1, Pallas kernels, on_device(): pl.pallas_call(dispatch_kernel, out_shape=slots, in_specs=[pl.BlockSpec(m...  2.23 us

profile of v3, /device:TPU:1, one launch (start us, length us, event | category | flops | bytes accessed | tf_op | source)
XLA Modules:
  0.0 88.0 jit_solution(8600532570050208590)
XLA Ops:
  0.0 0.0 slice-start
  0.0 0.0 slice-start.2
  0.0 0.0 slice-start.4
  0.0 0.0 slice-start.1
  0.0 0.0 slice-start.3
  0.0 0.0 slice-start.5
  0.0 2.2 %dispatch.1 = bf16[1024,1024]{1,0:T(8,128)(2,1)S(1)} custom-call(s32[8,16]{1,0:T(8,128)} %bitcast.22, bf16[16,4096]{1,0:T(8,128)(2,1)} %tok_hbm.1), custom_call_target="tpu_custom_call" | custom-call | flops 20000000000 | bytes 100000000 | tf_op jit(solution)/shard_map/dispatch/pallas_call | solution.py:143
  2.3 0.0 copy-start
  2.3 0.0 copy-start.1
  2.3 41.9 %all_to_all.10 = bf16[128,8,1024]{2,1,0:T(8,128)(2,1)S(1)} all-to-all(bf16[128,8,1024]{2,1,0:T(8,128)(2,1)S(1)} %bitcast.21), channel_id=1, replica_groups=mesh['node'=32,'local'=4] {'node','local'}, dimensions={0} | all-to-all | bytes 4194304 | tf_op jit(solution)/shard_map/all_to_all | solution.py:138
  44.2 0.0 slice-done
  44.2 0.0 slice-done.2
  44.2 0.0 slice-done.4
  44.2 0.0 slice-done.1
  44.2 0.0 slice-done.3
  44.2 0.0 slice-done.5
  44.2 0.0 copy-done
  44.2 0.0 copy-done.1
  44.3 8.3 %expert.1 = (bf16[1024,1024]{1,0:T(8,128)(2,1)S(1)}, bf16[192,1024]{1,0:T(8,128)(2,1)S(1)}) custom-call(s32[8,16]{1,0:T(8,128)S(1)} %bitcast.23, f32[8,16]{1,0:T(8,128)S(1)} %bitcast.24, bf16[1024,1024]{1,0:T(8,128)(2,1)S(1)} %bitcast.9, bf16[4096,1024]{1,0:T(8,128)(2,1)S(1)} %bitcast.13, bf16[4096,1024]{1,0:T(8,128)(2,1)S(1)} %bitcast.16, ...), custom_call_target="tpu_custom_call" | custom-call | flops 6499999744 | bytes 30000000 | tf_op jit(solution)/shard_map/expert/pallas_call | solution.py:157
  52.6 34.2 %all_to_all.11 = bf16[128,8,1024]{2,1,0:T(8,128)(2,1)S(1)} all-to-all(bf16[128,8,1024]{2,1,0:T(8,128)(2,1)S(1)} %bitcast.20), channel_id=1, replica_groups=mesh['node'=32,'local'=4] {'node','local'}, dimensions={0} | all-to-all | bytes 4194304 | tf_op jit(solution)/shard_map/all_to_all | solution.py:138
  86.8 1.2 %combine.1 = bf16[16,4096]{1,0:T(8,128)(2,1)} custom-call(bf16[192,1024]{1,0:T(8,128)(2,1)S(1)} %get-tuple-element.7.weights_ref, bf16[1024,1024]{1,0:T(8,128)(2,1)S(1)} %bitcast.10), custom_call_target="tpu_custom_call" | custom-call | tf_op jit(solution)/shard_map/combine/pallas_call | solution.py:170
  (3 shorter events, 0.0 us)
Async XLA Ops:
  0.0 44.2 %slice-start = ((s8[8388608]{0:T(1024)(128)(4,1)}), s8[4194304]{0:T(1024)(128)(4,1)S(1)}, s32[]{:S(2)}) async-start(s8[8388608]{0:T(1024)(128)(4,1)} %bitcast.11), calls=%async_computation.2 | async-start | bytes 8388608
  0.0 44.2 %slice-start.2 = ((s8[8388608]{0:T(1024)(128)(4,1)}), s8[4194304]{0:T(1024)(128)(4,1)S(1)}, s32[]{:S(2)}) async-start(s8[8388608]{0:T(1024)(128)(4,1)} %bitcast.14), calls=%async_computation.4 | async-start | bytes 8388608
  0.0 44.2 %slice-start.4 = ((s8[8388608]{0:T(1024)(128)(4,1)}), s8[4194304]{0:T(1024)(128)(4,1)S(1)}, s32[]{:S(2)}) async-start(s8[8388608]{0:T(1024)(128)(4,1)} %bitcast.17), calls=%async_computation.6 | async-start | bytes 8388608
  0.0 44.2 %slice-start.1 = ((s8[8388608]{0:T(1024)(128)(4,1)}), s8[4194304]{0:T(1024)(128)(4,1)S(1)}, s32[]{:S(2)}) async-start(s8[8388608]{0:T(1024)(128)(4,1)} %bitcast.11), calls=%async_computation.3 | async-start | bytes 8388608
  0.0 44.2 %slice-start.3 = ((s8[8388608]{0:T(1024)(128)(4,1)}), s8[4194304]{0:T(1024)(128)(4,1)S(1)}, s32[]{:S(2)}) async-start(s8[8388608]{0:T(1024)(128)(4,1)} %bitcast.14), calls=%async_computation.5 | async-start | bytes 8388608
  0.0 44.2 %slice-start.5 = ((s8[8388608]{0:T(1024)(128)(4,1)}), s8[4194304]{0:T(1024)(128)(4,1)S(1)}, s32[]{:S(2)}) async-start(s8[8388608]{0:T(1024)(128)(4,1)} %bitcast.17), calls=%async_computation.7 | async-start | bytes 8388608
  2.3 41.9 %copy-start = (s32[16,8]{0,1:T(8,128)S(1)}, s32[16,8]{0,1:T(8,128)}, u32[]{:S(2)}) copy-start(s32[16,8]{0,1:T(8,128)} %param.7) | copy-start | bytes 1540
  2.3 41.9 %copy-start.1 = (f32[16,8]{0,1:T(8,128)S(1)}, f32[16,8]{0,1:T(8,128)}, u32[]{:S(2)}) copy-start(f32[16,8]{0,1:T(8,128)} %param.8) | copy-start | bytes 1540

commit v4 on v3

--- a/solution.py
+++ b/solution.py
@@ -18,33 +18,35 @@
     return [pl.BlockSpec(memory_space=pltpu.VMEM)] * count
 
 
-def lane_columns(wide_t):
+def columns(wide_t):
     top, toks = wide_t.shape
-    return jnp.concatenate([wide_t] * (128 // toks), axis=1).T[: PARTS * toks]
+    return jnp.concatenate([wide_t] * (128 // toks), axis=1).T[:toks]
 
 
 def routing(ids_t, values_t, experts):
     top, toks = ids_t.shape
-    shape = (PARTS * toks, experts * ROWS)
-    lane = lax.broadcasted_iota(jnp.int32, shape, 0)
+    shape = (toks, experts * ROWS)
     row = lax.broadcasted_iota(jnp.int32, shape, 1)
-    ids = lane_columns(ids_t)
+    ids = columns(ids_t)
     expert = row // ROWS
     named = [expert == ids[:, k : k + 1] for k in range(top)]
     member = functools.reduce(jnp.logical_or, named).astype(F32)
-    square = (PARTS * toks, PARTS * toks)
-    later = lax.broadcasted_iota(jnp.int32, square, 0)
-    sooner = lax.broadcasted_iota(jnp.int32, square, 1)
-    earlier = ((later // toks == sooner // toks) & (sooner < later)).astype(F32).astype(BF16)
+    later = lax.broadcasted_iota(jnp.int32, (toks, toks), 0)
+    sooner = lax.broadcasted_iota(jnp.int32, (toks, toks), 1)
+    earlier = (sooner < later).astype(F32).astype(BF16)
     before = jnp.dot(earlier, member.astype(BF16), preferred_element_type=F32)
-    slot = ((row // PARTS) % CAP).astype(F32)
-    own = (before == slot) & (row % PARTS == lane // toks)
+    own = before == ((row // PARTS) % CAP).astype(F32)
     if values_t is not None:
-        values = lane_columns(values_t)
+        values = columns(values_t)
         member = jnp.zeros(shape, F32)
         for k, here in enumerate(named):
             member = jnp.where(here, values[:, k : k + 1], member)
     return jnp.where(own, member, 0.0)
+
+
+def by_part(filled):
+    part_of = lax.broadcasted_iota(jnp.int32, filled.shape, 1) % PARTS
+    return jnp.concatenate([jnp.where(part_of == part, filled, 0.0) for part in range(PARTS)], axis=0).astype(BF16)
 
 
 def dispatch_kernel(ids_hbm, tok_hbm, out_ref, ids_ref, tok_parts, sems):
@@ -59,7 +61,7 @@
         loads.append(pltpu.make_async_copy(source, tok_parts.at[pl.ds(part * toks, toks), :], sems.at[part]))
         loads[-1].start()
     ids_load.wait()
-    select = routing(ids_ref[...], None, experts).astype(BF16)
+    select = by_part(routing(ids_ref[...], None, experts))
     for load in loads:
         load.wait()
     out_ref[...] = lax.dot_general(
@@ -71,9 +73,9 @@
     lanes = out_ref.shape[0] // 3
     rest = routing(ids_t, gates_t, out_ref.shape[1] // ROWS)
     for term in range(3):
-        piece = rest.astype(BF16)
-        out_ref[term * lanes : (term + 1) * lanes, :] = piece
-        rest = rest - piece.astype(F32)
+        piece = rest.astype(BF16).astype(F32)
+        out_ref[term * lanes : (term + 1) * lanes, :] = by_part(piece)
+        rest = rest - piece
 
 
 def combine_kernel(weights_ref, rows_ref, out_ref):

time: 88.1 us -> 87.7 us (level)
  no operation moved by 1% of the time
where the time goes in v4:
time: 87.7 us; the launch traced here: 87.6 us
  blocking collectives  76.1 us (87%)
  Pallas kernels  11.4 us (13%)
    all_to_all x2, blocking collectives, exchange(): lax.all_to_all(rows.reshape(experts, ROWS, wide), ('node', 'local'), spli...  76.1 us
    pallas_call x1, Pallas kernels, on_device(): pl.pallas_call(expert_kernel, out_shape=[slots, jax.ShapeDtypeStruct((3 *...  8.13 us
    pallas_call x1, Pallas kernels, on_device(): pl.pallas_call(dispatch_kernel, out_shape=slots, in_specs=[pl.BlockSpec(m...  2.02 us

profile of v4, /device:TPU:1, one launch (start us, length us, event | category | flops | bytes accessed | tf_op | source)
XLA Modules:
  0.0 87.6 jit_solution(3410121228039690139)
XLA Ops:
  0.0 0.0 slice-start
  0.0 0.0 slice-start.2
  0.0 0.0 slice-start.4
  0.0 0.0 slice-start.1
  0.0 0.0 slice-start.3
  0.0 0.0 slice-start.5
  0.0 2.0 %dispatch.1 = bf16[1024,1024]{1,0:T(8,128)(2,1)S(1)} custom-call(s32[8,16]{1,0:T(8,128)} %bitcast.22, bf16[16,4096]{1,0:T(8,128)(2,1)} %tok_hbm.1), custom_call_target="tpu_custom_call" | custom-call | flops 20000000000 | bytes 100000000 | tf_op jit(solution)/shard_map/dispatch/pallas_call | solution.py:145
  2.1 0.0 copy-start
  2.1 0.0 copy-start.1
  2.1 41.9 %all_to_all.10 = bf16[128,8,1024]{2,1,0:T(8,128)(2,1)S(1)} all-to-all(bf16[128,8,1024]{2,1,0:T(8,128)(2,1)S(1)} %bitcast.21), channel_id=1, replica_groups=mesh['node'=32,'local'=4] {'node','local'}, dimensions={0} | all-to-all | bytes 4194304 | tf_op jit(solution)/shard_map/all_to_all | solution.py:140
  44.0 0.0 slice-done
  44.0 0.0 slice-done.2
  44.0 0.0 slice-done.4
  44.0 0.0 slice-done.1
  44.0 0.0 slice-done.3
  44.0 0.0 slice-done.5
  44.0 0.0 copy-done
  44.0 0.0 copy-done.1
  44.0 8.1 %expert.1 = (bf16[1024,1024]{1,0:T(8,128)(2,1)S(1)}, bf16[192,1024]{1,0:T(8,128)(2,1)S(1)}) custom-call(s32[8,16]{1,0:T(8,128)S(1)} %bitcast.23, f32[8,16]{1,0:T(8,128)S(1)} %bitcast.24, bf16[1024,1024]{1,0:T(8,128)(2,1)S(1)} %bitcast.9, bf16[4096,1024]{1,0:T(8,128)(2,1)S(1)} %bitcast.13, bf16[4096,1024]{1,0:T(8,128)(2,1)S(1)} %bitcast.16, ...), custom_call_target="tpu_custom_call" | custom-call | flops 6499999744 | bytes 30000000 | tf_op jit(solution)/shard_map/expert/pallas_call | solution.py:159
  52.2 34.2 %all_to_all.11 = bf16[128,8,1024]{2,1,0:T(8,128)(2,1)S(1)} all-to-all(bf16[128,8,1024]{2,1,0:T(8,128)(2,1)S(1)} %bitcast.20), channel_id=1, replica_groups=mesh['node'=32,'local'=4] {'node','local'}, dimensions={0} | all-to-all | bytes 4194304 | tf_op jit(solution)/shard_map/all_to_all | solution.py:140
  86.4 1.2 %combine.1 = bf16[16,4096]{1,0:T(8,128)(2,1)} custom-call(bf16[192,1024]{1,0:T(8,128)(2,1)S(1)} %get-tuple-element.7.weights_ref, bf16[1024,1024]{1,0:T(8,128)(2,1)S(1)} %bitcast.10), custom_call_target="tpu_custom_call" | custom-call | tf_op jit(solution)/shard_map/combine/pallas_call | solution.py:172
  (3 shorter events, 0.0 us)
Async XLA Ops:
  0.0 44.0 %slice-start = ((s8[8388608]{0:T(1024)(128)(4,1)}), s8[4194304]{0:T(1024)(128)(4,1)S(1)}, s32[]{:S(2)}) async-start(s8[8388608]{0:T(1024)(128)(4,1)} %bitcast.11), calls=%async_computation.2 | async-start | bytes 8388608
  0.0 44.0 %slice-start.2 = ((s8[8388608]{0:T(1024)(128)(4,1)}), s8[4194304]{0:T(1024)(128)(4,1)S(1)}, s32[]{:S(2)}) async-start(s8[8388608]{0:T(1024)(128)(4,1)} %bitcast.14), calls=%async_computation.4 | async-start | bytes 8388608
  0.0 44.0 %slice-start.4 = ((s8[8388608]{0:T(1024)(128)(4,1)}), s8[4194304]{0:T(1024)(128)(4,1)S(1)}, s32[]{:S(2)}) async-start(s8[8388608]{0:T(1024)(128)(4,1)} %bitcast.17), calls=%async_computation.6 | async-start | bytes 8388608
  0.0 44.0 %slice-start.1 = ((s8[8388608]{0:T(1024)(128)(4,1)}), s8[4194304]{0:T(1024)(128)(4,1)S(1)}, s32[]{:S(2)}) async-start(s8[8388608]{0:T(1024)(128)(4,1)} %bitcast.11), calls=%async_computation.3 | async-start | bytes 8388608
  0.0 44.0 %slice-start.3 = ((s8[8388608]{0:T(1024)(128)(4,1)}), s8[4194304]{0:T(1024)(128)(4,1)S(1)}, s32[]{:S(2)}) async-start(s8[8388608]{0:T(1024)(128)(4,1)} %bitcast.14), calls=%async_computation.5 | async-start | bytes 8388608
  0.0 44.0 %slice-start.5 = ((s8[8388608]{0:T(1024)(128)(4,1)}), s8[4194304]{0:T(1024)(128)(4,1)S(1)}, s32[]{:S(2)}) async-start(s8[8388608]{0:T(1024)(128)(4,1)} %bitcast.17), calls=%async_computation.7 | async-start | bytes 8388608
  2.1 41.9 %copy-start = (s32[16,8]{0,1:T(8,128)S(1)}, s32[16,8]{0,1:T(8,128)}, u32[]{:S(2)}) copy-start(s32[16,8]{0,1:T(8,128)} %param.7) | copy-start | bytes 1540
  2.1 41.9 %copy-start.1 = (f32[16,8]{0,1:T(8,128)S(1)}, f32[16,8]{0,1:T(8,128)}, u32[]{:S(2)}) copy-start(f32[16,8]{0,1:T(8,128)} %param.8) | copy-start | bytes 1540

commit v5 on v4

--- a/solution.py
+++ b/solution.py
@@ -35,7 +35,7 @@
     sooner = lax.broadcasted_iota(jnp.int32, (toks, toks), 1)
     earlier = (sooner < later).astype(F32).astype(BF16)
     before = jnp.dot(earlier, member.astype(BF16), preferred_element_type=F32)
-    own = before == ((row // PARTS) % CAP).astype(F32)
+    own = before == (row % CAP).astype(F32)
     if values_t is not None:
         values = columns(values_t)
         member = jnp.zeros(shape, F32)
@@ -45,7 +45,7 @@
 
 
 def by_part(filled):
-    part_of = lax.broadcasted_iota(jnp.int32, filled.shape, 1) % PARTS
+    part_of = (lax.broadcasted_iota(jnp.int32, filled.shape, 1) % ROWS) // CAP
     return jnp.concatenate([jnp.where(part_of == part, filled, 0.0) for part in range(PARTS)], axis=0).astype(BF16)
 
 
@@ -91,38 +91,53 @@
 def expert_kernel(ids_ref, gates_ref, rows_ref, gate_ref, up_ref, down_ref, out_ref, weights_ref, x, hidden):
     wide = rows_ref.shape[1]
     units = gate_ref.shape[1]
-    count = x.shape[0]
     chunk = 256
-    pieces = 256 // ROWS
-    first = lax.broadcasted_iota(jnp.int32, (256, 256), 0)
-    second = lax.broadcasted_iota(jnp.int32, (256, 256), 1)
-    ungroup = (second == (first % pieces) * ROWS + first // pieces).astype(F32).astype(BF16)
-    group = (first == (second % pieces) * ROWS + second // pieces).astype(F32).astype(BF16)
-    half = count // CAP
-    for b in range(rows_ref.shape[0] // 256):
-        spread = jnp.dot(ungroup, rows_ref[b * 256 : (b + 1) * 256, :], preferred_element_type=F32).astype(BF16)
-        for r in range(ROWS):
-            slot, part = r // PARTS, r % PARTS
-            start = slot * half + b * pieces
-            x[start : start + pieces, part * wide : (part + 1) * wide] = spread[r * pieces : (r + 1) * pieces]
-    for i in range(units // chunk):
+    pieces = chunk // ROWS
+    here = pieces * CAP
+    blocks = range(rows_ref.shape[0] // chunk)
+
+    def parts_of(block):
+        return rows_ref[block * chunk : (block + 1) * chunk, :].reshape(pieces, ROWS, wide)
+
+    def gather(part, which):
+        for b in which:
+            rows = parts_of(b)[:, part * CAP : (part + 1) * CAP, :].reshape(here, wide)
+            x[b * here : (b + 1) * here, part * wide : (part + 1) * wide] = rows
+
+    def activate(cols, g, u):
+        hidden[:, cols] = (g / (1.0 + jnp.exp(-g)) * u).astype(BF16)
+
+    gather(0, blocks)
+    cols = slice(0, chunk)
+    g = u = None
+    for part in range(PARTS):
+        depth = slice(part * wide, (part + 1) * wide)
+        gate_term = jnp.dot(x[:, depth], gate_ref[depth, cols], preferred_element_type=F32)
+        if part + 1 < PARTS:
+            gather(part + 1, blocks[: len(blocks) // 2])
+        up_term = jnp.dot(x[:, depth], up_ref[depth, cols], preferred_element_type=F32)
+        if part + 1 < PARTS:
+            gather(part + 1, blocks[len(blocks) // 2 :])
+        g = gate_term if g is None else g + gate_term
+        u = up_term if u is None else u + up_term
+    activate(cols, g, u)
+    for i in range(1, units // chunk):
         cols = slice(i * chunk, (i + 1) * chunk)
         g = jnp.dot(x[...], gate_ref[:, cols], preferred_element_type=F32)
         u = jnp.dot(x[...], up_ref[:, cols], preferred_element_type=F32)
-        hidden[:, cols] = (g / (1.0 + jnp.exp(-g)) * u).astype(BF16)
-        if i == 0:
-            combine_weights(ids_ref[...], gates_ref[...], weights_ref)
+        activate(cols, g, u)
+    combine_weights(ids_ref[...], gates_ref[...], weights_ref)
     for part in range(PARTS):
         cols = slice(part * wide, (part + 1) * wide)
         x[:, cols] = jnp.dot(hidden[...], down_ref[:, cols], preferred_element_type=F32).astype(BF16)
-    for b in range(rows_ref.shape[0] // 256):
-        parts = []
-        for r in range(ROWS):
-            slot, part = r // PARTS, r % PARTS
-            start = slot * half + b * pieces
-            parts.append(x[start : start + pieces, part * wide : (part + 1) * wide])
-        out_ref[b * 256 : (b + 1) * 256, :] = jnp.dot(
-            group, jnp.concatenate(parts, axis=0), preferred_element_type=F32
+    first = lax.broadcasted_iota(jnp.int32, (chunk, chunk), 0)
+    second = lax.broadcasted_iota(jnp.int32, (chunk, chunk), 1)
+    source = ((first % ROWS) // CAP) * here + (first // ROWS) * CAP + first % CAP
+    group = (second == source).astype(F32).astype(BF16)
+    for b in blocks:
+        own = [x[b * here : (b + 1) * here, part * wide : (part + 1) * wide] for part in range(PARTS)]
+        out_ref[b * chunk : (b + 1) * chunk, :] = jnp.dot(
+            group, jnp.concatenate(own, axis=0), preferred_element_type=F32
         ).astype(BF16)
 
 

time: 87.7 us -> 87.5 us (level)
  no operation moved by 1% of the time
where the time goes in v5:
time: 87.5 us; the launch traced here: 87.4 us
  blocking collectives  76 us (87%)
  Pallas kernels  11.2 us (13%)
    all_to_all x2, blocking collectives, exchange(): lax.all_to_all(rows.reshape(experts, ROWS, wide), ('node', 'local'), spli...  76 us
    pallas_call x1, Pallas kernels, on_device(): pl.pallas_call(expert_kernel, out_shape=[slots, jax.ShapeDtypeStruct((3 *...  7.95 us
    pallas_call x1, Pallas kernels, on_device(): pl.pallas_call(dispatch_kernel, out_shape=slots, in_specs=[pl.BlockSpec(m...  2.02 us

profile of v5, /device:TPU:1, one launch (start us, length us, event | category | flops | bytes accessed | tf_op | source)
XLA Modules:
  0.0 87.4 jit_solution(7247380770648643246)
XLA Ops:
  0.0 0.0 slice-start
  0.0 0.0 slice-start.2
  0.0 0.0 slice-start.4
  0.0 0.0 slice-start.1
  0.0 0.0 slice-start.3
  0.0 0.0 slice-start.5
  0.0 2.0 %dispatch.1 = bf16[1024,1024]{1,0:T(8,128)(2,1)S(1)} custom-call(s32[8,16]{1,0:T(8,128)} %bitcast.22, bf16[16,4096]{1,0:T(8,128)(2,1)} %tok_hbm.1), custom_call_target="tpu_custom_call" | custom-call | flops 20000000000 | bytes 100000000 | tf_op jit(solution)/shard_map/dispatch/pallas_call | solution.py:160
  2.1 0.0 copy-start
  2.1 0.0 copy-start.1
  2.1 41.9 %all_to_all.10 = bf16[128,8,1024]{2,1,0:T(8,128)(2,1)S(1)} all-to-all(bf16[128,8,1024]{2,1,0:T(8,128)(2,1)S(1)} %bitcast.21), channel_id=1, replica_groups=mesh['node'=32,'local'=4] {'node','local'}, dimensions={0} | all-to-all | bytes 4194304 | tf_op jit(solution)/shard_map/all_to_all | solution.py:155
  44.0 0.0 slice-done
  44.0 0.0 slice-done.2
  44.0 0.0 slice-done.4
  44.0 0.0 slice-done.1
  44.0 0.0 slice-done.3
  44.0 0.0 slice-done.5
  44.0 0.0 copy-done
  44.0 0.0 copy-done.1
  44.0 7.9 %expert.1 = (bf16[1024,1024]{1,0:T(8,128)(2,1)S(1)}, bf16[192,1024]{1,0:T(8,128)(2,1)S(1)}) custom-call(s32[8,16]{1,0:T(8,128)S(1)} %bitcast.23, f32[8,16]{1,0:T(8,128)S(1)} %bitcast.24, bf16[1024,1024]{1,0:T(8,128)(2,1)S(1)} %bitcast.9, bf16[4096,1024]{1,0:T(8,128)(2,1)S(1)} %bitcast.13, bf16[4096,1024]{1,0:T(8,128)(2,1)S(1)} %bitcast.16, ...), custom_call_target="tpu_custom_call" | custom-call | flops 6499999744 | bytes 30000000 | tf_op jit(solution)/shard_map/expert/pallas_call | solution.py:174
  52.0 34.2 %all_to_all.11 = bf16[128,8,1024]{2,1,0:T(8,128)(2,1)S(1)} all-to-all(bf16[128,8,1024]{2,1,0:T(8,128)(2,1)S(1)} %bitcast.20), channel_id=1, replica_groups=mesh['node'=32,'local'=4] {'node','local'}, dimensions={0} | all-to-all | bytes 4194304 | tf_op jit(solution)/shard_map/all_to_all | solution.py:155
  86.2 1.2 %combine.1 = bf16[16,4096]{1,0:T(8,128)(2,1)} custom-call(bf16[192,1024]{1,0:T(8,128)(2,1)S(1)} %get-tuple-element.7.weights_ref, bf16[1024,1024]{1,0:T(8,128)(2,1)S(1)} %bitcast.10), custom_call_target="tpu_custom_call" | custom-call | tf_op jit(solution)/shard_map/combine/pallas_call | solution.py:187
  (3 shorter events, 0.0 us)
Async XLA Ops:
  0.0 44.0 %slice-start = ((s8[8388608]{0:T(1024)(128)(4,1)}), s8[4194304]{0:T(1024)(128)(4,1)S(1)}, s32[]{:S(2)}) async-start(s8[8388608]{0:T(1024)(128)(4,1)} %bitcast.11), calls=%async_computation.2 | async-start | bytes 8388608
  0.0 44.0 %slice-start.2 = ((s8[8388608]{0:T(1024)(128)(4,1)}), s8[4194304]{0:T(1024)(128)(4,1)S(1)}, s32[]{:S(2)}) async-start(s8[8388608]{0:T(1024)(128)(4,1)} %bitcast.14), calls=%async_computation.4 | async-start | bytes 8388608
  0.0 44.0 %slice-start.4 = ((s8[8388608]{0:T(1024)(128)(4,1)}), s8[4194304]{0:T(1024)(128)(4,1)S(1)}, s32[]{:S(2)}) async-start(s8[8388608]{0:T(1024)(128)(4,1)} %bitcast.17), calls=%async_computation.6 | async-start | bytes 8388608
  0.0 44.0 %slice-start.1 = ((s8[8388608]{0:T(1024)(128)(4,1)}), s8[4194304]{0:T(1024)(128)(4,1)S(1)}, s32[]{:S(2)}) async-start(s8[8388608]{0:T(1024)(128)(4,1)} %bitcast.11), calls=%async_computation.3 | async-start | bytes 8388608
  0.0 44.0 %slice-start.3 = ((s8[8388608]{0:T(1024)(128)(4,1)}), s8[4194304]{0:T(1024)(128)(4,1)S(1)}, s32[]{:S(2)}) async-start(s8[8388608]{0:T(1024)(128)(4,1)} %bitcast.14), calls=%async_computation.5 | async-start | bytes 8388608
  0.0 44.0 %slice-start.5 = ((s8[8388608]{0:T(1024)(128)(4,1)}), s8[4194304]{0:T(1024)(128)(4,1)S(1)}, s32[]{:S(2)}) async-start(s8[8388608]{0:T(1024)(128)(4,1)} %bitcast.17), calls=%async_computation.7 | async-start | bytes 8388608
  2.1 41.9 %copy-start = (s32[16,8]{0,1:T(8,128)S(1)}, s32[16,8]{0,1:T(8,128)}, u32[]{:S(2)}) copy-start(s32[16,8]{0,1:T(8,128)} %param.7) | copy-start | bytes 1540
  2.1 41.9 %copy-start.1 = (f32[16,8]{0,1:T(8,128)S(1)}, f32[16,8]{0,1:T(8,128)}, u32[]{:S(2)}) copy-start(f32[16,8]{0,1:T(8,128)} %param.8) | copy-start | bytes 1540

commit v6 on v4

--- a/solution.py
+++ b/solution.py
@@ -23,24 +23,22 @@
     return jnp.concatenate([wide_t] * (128 // toks), axis=1).T[:toks]
 
 
-def routing(ids_t, values_t, experts):
+def named_rows(ids_t, rows):
     top, toks = ids_t.shape
-    shape = (toks, experts * ROWS)
-    row = lax.broadcasted_iota(jnp.int32, shape, 1)
+    expert = lax.broadcasted_iota(jnp.int32, (toks, rows), 1) // ROWS
     ids = columns(ids_t)
-    expert = row // ROWS
-    named = [expert == ids[:, k : k + 1] for k in range(top)]
-    member = functools.reduce(jnp.logical_or, named).astype(F32)
+    return [expert == ids[:, k : k + 1] for k in range(top)]
+
+
+def routing(ids_t, experts):
+    toks = ids_t.shape[1]
+    member = functools.reduce(jnp.logical_or, named_rows(ids_t, experts * ROWS)).astype(F32)
     later = lax.broadcasted_iota(jnp.int32, (toks, toks), 0)
     sooner = lax.broadcasted_iota(jnp.int32, (toks, toks), 1)
     earlier = (sooner < later).astype(F32).astype(BF16)
     before = jnp.dot(earlier, member.astype(BF16), preferred_element_type=F32)
+    row = lax.broadcasted_iota(jnp.int32, member.shape, 1)
     own = before == ((row // PARTS) % CAP).astype(F32)
-    if values_t is not None:
-        values = columns(values_t)
-        member = jnp.zeros(shape, F32)
-        for k, here in enumerate(named):
-            member = jnp.where(here, values[:, k : k + 1], member)
     return jnp.where(own, member, 0.0)
 
 
@@ -49,7 +47,7 @@
     return jnp.concatenate([jnp.where(part_of == part, filled, 0.0) for part in range(PARTS)], axis=0).astype(BF16)
 
 
-def dispatch_kernel(ids_hbm, tok_hbm, out_ref, ids_ref, tok_parts, sems):
+def dispatch_kernel(ids_hbm, tok_hbm, out_ref, filled_ref, ids_ref, tok_parts, sems):
     toks = tok_hbm.shape[0]
     wide = tok_parts.shape[1]
     experts = out_ref.shape[0] // ROWS
@@ -61,7 +59,9 @@
         loads.append(pltpu.make_async_copy(source, tok_parts.at[pl.ds(part * toks, toks), :], sems.at[part]))
         loads[-1].start()
     ids_load.wait()
-    select = by_part(routing(ids_ref[...], None, experts))
+    filled = routing(ids_ref[...], experts)
+    filled_ref[...] = filled.astype(BF16)
+    select = by_part(filled)
     for load in loads:
         load.wait()
     out_ref[...] = lax.dot_general(
@@ -69,9 +69,13 @@
     ).astype(BF16)
 
 
-def combine_weights(ids_t, gates_t, out_ref):
+def combine_weights(ids_t, gates_t, filled, out_ref):
     lanes = out_ref.shape[0] // 3
-    rest = routing(ids_t, gates_t, out_ref.shape[1] // ROWS)
+    gates = columns(gates_t)
+    rest = jnp.zeros(filled.shape, F32)
+    for k, here in enumerate(named_rows(ids_t, filled.shape[1])):
+        rest = jnp.where(here, gates[:, k : k + 1], rest)
+    rest = rest * filled.astype(F32)
     for term in range(3):
         piece = rest.astype(BF16).astype(F32)
         out_ref[term * lanes : (term + 1) * lanes, :] = by_part(piece)
@@ -88,7 +92,7 @@
         out_ref[:, part * wide : (part + 1) * wide] = total[part * toks : (part + 1) * toks].astype(BF16)
 
 
-def expert_kernel(ids_ref, gates_ref, rows_ref, gate_ref, up_ref, down_ref, out_ref, weights_ref, x, hidden):
+def expert_kernel(ids_ref, gates_ref, filled_ref, rows_ref, gate_ref, up_ref, down_ref, out_ref, weights_ref, x, hidden):
     wide = rows_ref.shape[1]
     units = gate_ref.shape[1]
     count = x.shape[0]
@@ -111,7 +115,7 @@
         u = jnp.dot(x[...], up_ref[:, cols], preferred_element_type=F32)
         hidden[:, cols] = (g / (1.0 + jnp.exp(-g)) * u).astype(BF16)
         if i == 0:
-            combine_weights(ids_ref[...], gates_ref[...], weights_ref)
+            combine_weights(ids_ref[...], gates_ref[...], filled_ref[...], weights_ref)
     for part in range(PARTS):
         cols = slice(part * wide, (part + 1) * wide)
         x[:, cols] = jnp.dot(hidden[...], down_ref[:, cols], preferred_element_type=F32).astype(BF16)
@@ -142,11 +146,11 @@
         )
         return moved.reshape(piece_rows, wide)
 
-    outgoing = pl.pallas_call(
+    outgoing, filled = pl.pallas_call(
         dispatch_kernel,
-        out_shape=slots,
+        out_shape=[slots, jax.ShapeDtypeStruct((toks, piece_rows), BF16)],
         in_specs=[pl.BlockSpec(memory_space=pltpu.HBM)] * 2,
-        out_specs=pl.BlockSpec(memory_space=pltpu.VMEM),
+        out_specs=vmem(2),
         scratch_shapes=[
             pltpu.VMEM(ids_t.shape, jnp.int32),
             pltpu.VMEM((lanes, wide), BF16),
@@ -159,7 +163,7 @@
     finished, weights = pl.pallas_call(
         expert_kernel,
         out_shape=[slots, jax.ShapeDtypeStruct((3 * lanes, piece_rows), BF16)],
-        in_specs=vmem(6),
+        in_specs=vmem(7),
         out_specs=vmem(2),
         scratch_shapes=[
             pltpu.VMEM((experts * CAP, features), BF16),
@@ -168,7 +172,7 @@
         compiler_params=pltpu.CompilerParams(vmem_limit_bytes=16 << 20),
         cost_estimate=pl.CostEstimate(flops=6_500_000_000, bytes_accessed=30_000_000, transcendentals=0),
         name="expert",
-    )(ids_t, gates_t, exchange(outgoing), w_gate[0], w_up[0], w_down[0])
+    )(ids_t, gates_t, filled, exchange(outgoing), w_gate[0], w_up[0], w_down[0])
     return pl.pallas_call(
         combine_kernel,
         out_shape=jax.ShapeDtypeStruct((toks, features), BF16),

time: 87.7 us -> 87.6 us (level)
  no operation moved by 1% of the time
where the time goes in v6:
time: 87.6 us; the launch traced here: 87.5 us
  blocking collectives  76.1 us (87%)
  Pallas kernels  11.3 us (13%)
    all_to_all x2, blocking collectives, exchange(): lax.all_to_all(rows.reshape(experts, ROWS, wide), ('node', 'local'), spli...  76.1 us
    pallas_call x1, Pallas kernels, on_device(): pl.pallas_call(expert_kernel, out_shape=[slots, jax.ShapeDtypeStruct((3 *...  8.02 us
    pallas_call x1, Pallas kernels, on_device(): pl.pallas_call(dispatch_kernel, out_shape=[slots, jax.ShapeDtypeStruct((t...  2.02 us

profile of v6, /device:TPU:1, one launch (start us, length us, event | category | flops | bytes accessed | tf_op | source)
XLA Modules:
  0.0 87.5 jit_solution(3604223221044433904)
XLA Ops:
  0.0 0.0 slice-start
  0.0 0.0 slice-start.2
  0.0 0.0 slice-start.4
  0.0 0.0 slice-start.1
  0.0 0.0 slice-start.3
  0.0 0.0 slice-start.5
  0.0 2.0 %dispatch.1 = (bf16[1024,1024]{1,0:T(8,128)(2,1)S(1)}, bf16[16,1024]{1,0:T(8,128)(2,1)S(1)}) custom-call(s32[8,16]{1,0:T(8,128)} %bitcast.22, bf16[16,4096]{1,0:T(8,128)(2,1)} %tok_hbm.1), custom_call_target="tpu_custom_call" | custom-call | flops 20000000000 | bytes 100000000 | tf_op jit(solution)/shard_map/dispatch/pallas_call | solution.py:149
  2.1 0.0 copy-start
  2.1 0.0 copy-start.1
  2.1 41.9 %all_to_all.10 = bf16[128,8,1024]{2,1,0:T(8,128)(2,1)S(1)} all-to-all(bf16[128,8,1024]{2,1,0:T(8,128)(2,1)S(1)} %bitcast.21), channel_id=1, replica_groups=mesh['node'=32,'local'=4] {'node','local'}, dimensions={0} | all-to-all | bytes 4194304 | tf_op jit(solution)/shard_map/all_to_all | solution.py:144
  44.0 0.0 slice-done
  44.0 0.0 slice-done.2
  44.0 0.0 slice-done.4
  44.0 0.0 slice-done.1
  44.0 0.0 slice-done.3
  44.0 0.0 slice-done.5
  44.0 0.0 copy-done
  44.0 0.0 copy-done.1
  44.0 8.0 %expert.1 = (bf16[1024,1024]{1,0:T(8,128)(2,1)S(1)}, bf16[192,1024]{1,0:T(8,128)(2,1)S(1)}) custom-call(s32[8,16]{1,0:T(8,128)S(1)} %bitcast.23, f32[8,16]{1,0:T(8,128)S(1)} %bitcast.24, bf16[16,1024]{1,0:T(8,128)(2,1)S(1)} %get-tuple-element.9.filled_ref, bf16[1024,1024]{1,0:T(8,128)(2,1)S(1)} %bitcast.18, bf16[4096,1024]{1,0:T(8,128)(2,1)S(1)} %bitcast.11, ...), custom_call_target="tpu_custom_call" | custom-call | flops 6499999744 | bytes 30000000 | tf_op jit(solution)/shard_map/expert/pallas_call | solution.py:163
  52.1 34.2 %all_to_all.11 = bf16[128,8,1024]{2,1,0:T(8,128)(2,1)S(1)} all-to-all(bf16[128,8,1024]{2,1,0:T(8,128)(2,1)S(1)} %bitcast.20), channel_id=1, replica_groups=mesh['node'=32,'local'=4] {'node','local'}, dimensions={0} | all-to-all | bytes 4194304 | tf_op jit(solution)/shard_map/all_to_all | solution.py:144
  86.3 1.2 %combine.1 = bf16[16,4096]{1,0:T(8,128)(2,1)} custom-call(bf16[192,1024]{1,0:T(8,128)(2,1)S(1)} %get-tuple-element.11.weights_ref, bf16[1024,1024]{1,0:T(8,128)(2,1)S(1)} %bitcast.19), custom_call_target="tpu_custom_call" | custom-call | tf_op jit(solution)/shard_map/combine/pallas_call | solution.py:176
  (3 shorter events, 0.0 us)
Async XLA Ops:
  0.0 44.0 %slice-start = ((s8[8388608]{0:T(1024)(128)(4,1)}), s8[4194304]{0:T(1024)(128)(4,1)S(1)}, s32[]{:S(2)}) async-start(s8[8388608]{0:T(1024)(128)(4,1)} %bitcast.9), calls=%async_computation.2 | async-start | bytes 8388608
  0.0 44.0 %slice-start.2 = ((s8[8388608]{0:T(1024)(128)(4,1)}), s8[4194304]{0:T(1024)(128)(4,1)S(1)}, s32[]{:S(2)}) async-start(s8[8388608]{0:T(1024)(128)(4,1)} %bitcast.12), calls=%async_computation.4 | async-start | bytes 8388608
  0.0 44.0 %slice-start.4 = ((s8[8388608]{0:T(1024)(128)(4,1)}), s8[4194304]{0:T(1024)(128)(4,1)S(1)}, s32[]{:S(2)}) async-start(s8[8388608]{0:T(1024)(128)(4,1)} %bitcast.15), calls=%async_computation.6 | async-start | bytes 8388608
  0.0 44.0 %slice-start.1 = ((s8[8388608]{0:T(1024)(128)(4,1)}), s8[4194304]{0:T(1024)(128)(4,1)S(1)}, s32[]{:S(2)}) async-start(s8[8388608]{0:T(1024)(128)(4,1)} %bitcast.9), calls=%async_computation.3 | async-start | bytes 8388608
  0.0 44.0 %slice-start.3 = ((s8[8388608]{0:T(1024)(128)(4,1)}), s8[4194304]{0:T(1024)(128)(4,1)S(1)}, s32[]{:S(2)}) async-start(s8[8388608]{0:T(1024)(128)(4,1)} %bitcast.12), calls=%async_computation.5 | async-start | bytes 8388608
  0.0 44.0 %slice-start.5 = ((s8[8388608]{0:T(1024)(128)(4,1)}), s8[4194304]{0:T(1024)(128)(4,1)S(1)}, s32[]{:S(2)}) async-start(s8[8388608]{0:T(1024)(128)(4,1)} %bitcast.15), calls=%async_computation.7 | async-start | bytes 8388608
  2.1 41.9 %copy-start = (s32[16,8]{0,1:T(8,128)S(1)}, s32[16,8]{0,1:T(8,128)}, u32[]{:S(2)}) copy-start(s32[16,8]{0,1:T(8,128)} %param.7) | copy-start | bytes 1540
  2.1 41.9 %copy-start.1 = (f32[16,8]{0,1:T(8,128)S(1)}, f32[16,8]{0,1:T(8,128)}, u32[]{:S(2)}) copy-start(f32[16,8]{0,1:T(8,128)} %param.8) | copy-start | bytes 1540

commit v7 on v5

--- a/solution.py
+++ b/solution.py
@@ -23,24 +23,22 @@
     return jnp.concatenate([wide_t] * (128 // toks), axis=1).T[:toks]
 
 
-def routing(ids_t, values_t, experts):
+def named_rows(ids_t, rows):
     top, toks = ids_t.shape
-    shape = (toks, experts * ROWS)
-    row = lax.broadcasted_iota(jnp.int32, shape, 1)
+    expert = lax.broadcasted_iota(jnp.int32, (toks, rows), 1) // ROWS
     ids = columns(ids_t)
-    expert = row // ROWS
-    named = [expert == ids[:, k : k + 1] for k in range(top)]
-    member = functools.reduce(jnp.logical_or, named).astype(F32)
+    return [expert == ids[:, k : k + 1] for k in range(top)]
+
+
+def routing(ids_t, experts):
+    toks = ids_t.shape[1]
+    member = functools.reduce(jnp.logical_or, named_rows(ids_t, experts * ROWS)).astype(F32)
     later = lax.broadcasted_iota(jnp.int32, (toks, toks), 0)
     sooner = lax.broadcasted_iota(jnp.int32, (toks, toks), 1)
     earlier = (sooner < later).astype(F32).astype(BF16)
     before = jnp.dot(earlier, member.astype(BF16), preferred_element_type=F32)
+    row = lax.broadcasted_iota(jnp.int32, member.shape, 1)
     own = before == (row % CAP).astype(F32)
-    if values_t is not None:
-        values = columns(values_t)
-        member = jnp.zeros(shape, F32)
-        for k, here in enumerate(named):
-            member = jnp.where(here, values[:, k : k + 1], member)
     return jnp.where(own, member, 0.0)
 
 
@@ -49,7 +47,7 @@
     return jnp.concatenate([jnp.where(part_of == part, filled, 0.0) for part in range(PARTS)], axis=0).astype(BF16)
 
 
-def dispatch_kernel(ids_hbm, tok_hbm, out_ref, ids_ref, tok_parts, sems):
+def dispatch_kernel(ids_hbm, tok_hbm, out_ref, filled_ref, ids_ref, tok_parts, sems):
     toks = tok_hbm.shape[0]
     wide = tok_parts.shape[1]
     experts = out_ref.shape[0] // ROWS
@@ -61,7 +59,9 @@
         loads.append(pltpu.make_async_copy(source, tok_parts.at[pl.ds(part * toks, toks), :], sems.at[part]))
         loads[-1].start()
     ids_load.wait()
-    select = by_part(routing(ids_ref[...], None, experts))
+    filled = routing(ids_ref[...], experts)
+    filled_ref[...] = filled.astype(BF16)
+    select = by_part(filled)
     for load in loads:
         load.wait()
     out_ref[...] = lax.dot_general(
@@ -69,9 +69,13 @@
     ).astype(BF16)
 
 
-def combine_weights(ids_t, gates_t, out_ref):
+def combine_weights(ids_t, gates_t, filled, out_ref):
     lanes = out_ref.shape[0] // 3
-    rest = routing(ids_t, gates_t, out_ref.shape[1] // ROWS)
+    gates = columns(gates_t)
+    rest = jnp.zeros(filled.shape, F32)
+    for k, here in enumerate(named_rows(ids_t, filled.shape[1])):
+        rest = jnp.where(here, gates[:, k : k + 1], rest)
+    rest = rest * filled.astype(F32)
     for term in range(3):
         piece = rest.astype(BF16).astype(F32)
         out_ref[term * lanes : (term + 1) * lanes, :] = by_part(piece)
@@ -88,7 +92,7 @@
         out_ref[:, part * wide : (part + 1) * wide] = total[part * toks : (part + 1) * toks].astype(BF16)
 
 
-def expert_kernel(ids_ref, gates_ref, rows_ref, gate_ref, up_ref, down_ref, out_ref, weights_ref, x, hidden):
+def expert_kernel(ids_ref, gates_ref, filled_ref, rows_ref, gate_ref, up_ref, down_ref, out_ref, weights_ref, x, hidden):
     wide = rows_ref.shape[1]
     units = gate_ref.shape[1]
     chunk = 256
@@ -126,7 +130,7 @@
         g = jnp.dot(x[...], gate_ref[:, cols], preferred_element_type=F32)
         u = jnp.dot(x[...], up_ref[:, cols], preferred_element_type=F32)
         activate(cols, g, u)
-    combine_weights(ids_ref[...], gates_ref[...], weights_ref)
+    combine_weights(ids_ref[...], gates_ref[...], filled_ref[...], weights_ref)
     for part in range(PARTS):
         cols = slice(part * wide, (part + 1) * wide)
         x[:, cols] = jnp.dot(hidden[...], down_ref[:, cols], preferred_element_type=F32).astype(BF16)
@@ -157,11 +161,11 @@
         )
         return moved.reshape(piece_rows, wide)
 
-    outgoing = pl.pallas_call(
+    outgoing, filled = pl.pallas_call(
         dispatch_kernel,
-        out_shape=slots,
+        out_shape=[slots, jax.ShapeDtypeStruct((toks, piece_rows), BF16)],
         in_specs=[pl.BlockSpec(memory_space=pltpu.HBM)] * 2,
-        out_specs=pl.BlockSpec(memory_space=pltpu.VMEM),
+        out_specs=vmem(2),
         scratch_shapes=[
             pltpu.VMEM(ids_t.shape, jnp.int32),
             pltpu.VMEM((lanes, wide), BF16),
@@ -174,7 +178,7 @@
     finished, weights = pl.pallas_call(
         expert_kernel,
         out_shape=[slots, jax.ShapeDtypeStruct((3 * lanes, piece_rows), BF16)],
-        in_specs=vmem(6),
+        in_specs=vmem(7),
         out_specs=vmem(2),
         scratch_shapes=[
             pltpu.VMEM((experts * CAP, features), BF16),
@@ -183,7 +187,7 @@
         compiler_params=pltpu.CompilerParams(vmem_limit_bytes=16 << 20),
         cost_estimate=pl.CostEstimate(flops=6_500_000_000, bytes_accessed=30_000_000, transcendentals=0),
         name="expert",
-    )(ids_t, gates_t, exchange(outgoing), w_gate[0], w_up[0], w_down[0])
+    )(ids_t, gates_t, filled, exchange(outgoing), w_gate[0], w_up[0], w_down[0])
     return pl.pallas_call(
         combine_kernel,
         out_shape=jax.ShapeDtypeStruct((toks, features), BF16),

time: 87.5 us -> 87.5 us (level)
  no operation moved by 1% of the time
where the time goes in v7:
time: 87.5 us; the launch traced here: 87.3 us
  blocking collectives  76.1 us (87%)
  Pallas kernels  11.1 us (13%)
    all_to_all x2, blocking collectives, exchange(): lax.all_to_all(rows.reshape(experts, ROWS, wide), ('node', 'local'), spli...  76.1 us
    pallas_call x1, Pallas kernels, on_device(): pl.pallas_call(expert_kernel, out_shape=[slots, jax.ShapeDtypeStruct((3 *...  7.86 us
    pallas_call x1, Pallas kernels, on_device(): pl.pallas_call(dispatch_kernel, out_shape=[slots, jax.ShapeDtypeStruct((t...  2.02 us

profile of v7, /device:TPU:1, one launch (start us, length us, event | category | flops | bytes accessed | tf_op | source)
XLA Modules:
  0.0 87.3 jit_solution(10333048966136052951)
XLA Ops:
  0.0 0.0 slice-start
  0.0 0.0 slice-start.2
  0.0 0.0 slice-start.4
  0.0 0.0 slice-start.1
  0.0 0.0 slice-start.3
  0.0 0.0 slice-start.5
  0.0 2.0 %dispatch.1 = (bf16[1024,1024]{1,0:T(8,128)(2,1)S(1)}, bf16[16,1024]{1,0:T(8,128)(2,1)S(1)}) custom-call(s32[8,16]{1,0:T(8,128)} %bitcast.22, bf16[16,4096]{1,0:T(8,128)(2,1)} %tok_hbm.1), custom_call_target="tpu_custom_call" | custom-call | flops 20000000000 | bytes 100000000 | tf_op jit(solution)/shard_map/dispatch/pallas_call | solution.py:164
  2.1 0.0 copy-start
  2.1 0.0 copy-start.1
  2.1 41.9 %all_to_all.10 = bf16[128,8,1024]{2,1,0:T(8,128)(2,1)S(1)} all-to-all(bf16[128,8,1024]{2,1,0:T(8,128)(2,1)S(1)} %bitcast.21), channel_id=1, replica_groups=mesh['node'=32,'local'=4] {'node','local'}, dimensions={0} | all-to-all | bytes 4194304 | tf_op jit(solution)/shard_map/all_to_all | solution.py:159
  44.0 0.0 slice-done
  44.0 0.0 slice-done.2
  44.0 0.0 slice-done.4
  44.0 0.0 slice-done.1
  44.0 0.0 slice-done.3
  44.0 0.0 slice-done.5
  44.0 0.0 copy-done
  44.0 0.0 copy-done.1
  44.0 7.9 %expert.1 = (bf16[1024,1024]{1,0:T(8,128)(2,1)S(1)}, bf16[192,1024]{1,0:T(8,128)(2,1)S(1)}) custom-call(s32[8,16]{1,0:T(8,128)S(1)} %bitcast.23, f32[8,16]{1,0:T(8,128)S(1)} %bitcast.24, bf16[16,1024]{1,0:T(8,128)(2,1)S(1)} %get-tuple-element.9.filled_ref, bf16[1024,1024]{1,0:T(8,128)(2,1)S(1)} %bitcast.18, bf16[4096,1024]{1,0:T(8,128)(2,1)S(1)} %bitcast.11, ...), custom_call_target="tpu_custom_call" | custom-call | flops 6499999744 | bytes 30000000 | tf_op jit(solution)/shard_map/expert/pallas_call | solution.py:178
  51.9 34.2 %all_to_all.11 = bf16[128,8,1024]{2,1,0:T(8,128)(2,1)S(1)} all-to-all(bf16[128,8,1024]{2,1,0:T(8,128)(2,1)S(1)} %bitcast.20), channel_id=1, replica_groups=mesh['node'=32,'local'=4] {'node','local'}, dimensions={0} | all-to-all | bytes 4194304 | tf_op jit(solution)/shard_map/all_to_all | solution.py:159
  86.1 1.2 %combine.1 = bf16[16,4096]{1,0:T(8,128)(2,1)} custom-call(bf16[192,1024]{1,0:T(8,128)(2,1)S(1)} %get-tuple-element.11.weights_ref, bf16[1024,1024]{1,0:T(8,128)(2,1)S(1)} %bitcast.19), custom_call_target="tpu_custom_call" | custom-call | tf_op jit(solution)/shard_map/combine/pallas_call | solution.py:191
  (3 shorter events, 0.0 us)
Async XLA Ops:
  0.0 44.0 %slice-start = ((s8[8388608]{0:T(1024)(128)(4,1)}), s8[4194304]{0:T(1024)(128)(4,1)S(1)}, s32[]{:S(2)}) async-start(s8[8388608]{0:T(1024)(128)(4,1)} %bitcast.9), calls=%async_computation.2 | async-start | bytes 8388608
  0.0 44.0 %slice-start.2 = ((s8[8388608]{0:T(1024)(128)(4,1)}), s8[4194304]{0:T(1024)(128)(4,1)S(1)}, s32[]{:S(2)}) async-start(s8[8388608]{0:T(1024)(128)(4,1)} %bitcast.12), calls=%async_computation.4 | async-start | bytes 8388608
  0.0 44.0 %slice-start.4 = ((s8[8388608]{0:T(1024)(128)(4,1)}), s8[4194304]{0:T(1024)(128)(4,1)S(1)}, s32[]{:S(2)}) async-start(s8[8388608]{0:T(1024)(128)(4,1)} %bitcast.15), calls=%async_computation.6 | async-start | bytes 8388608
  0.0 44.0 %slice-start.1 = ((s8[8388608]{0:T(1024)(128)(4,1)}), s8[4194304]{0:T(1024)(128)(4,1)S(1)}, s32[]{:S(2)}) async-start(s8[8388608]{0:T(1024)(128)(4,1)} %bitcast.9), calls=%async_computation.3 | async-start | bytes 8388608
  0.0 44.0 %slice-start.3 = ((s8[8388608]{0:T(1024)(128)(4,1)}), s8[4194304]{0:T(1024)(128)(4,1)S(1)}, s32[]{:S(2)}) async-start(s8[8388608]{0:T(1024)(128)(4,1)} %bitcast.12), calls=%async_computation.5 | async-start | bytes 8388608
  0.0 44.0 %slice-start.5 = ((s8[8388608]{0:T(1024)(128)(4,1)}), s8[4194304]{0:T(1024)(128)(4,1)S(1)}, s32[]{:S(2)}) async-start(s8[8388608]{0:T(1024)(128)(4,1)} %bitcast.15), calls=%async_computation.7 | async-start | bytes 8388608
  2.1 41.9 %copy-start = (s32[16,8]{0,1:T(8,128)S(1)}, s32[16,8]{0,1:T(8,128)}, u32[]{:S(2)}) copy-start(s32[16,8]{0,1:T(8,128)} %param.7) | copy-start | bytes 1540
  2.1 41.9 %copy-start.1 = (f32[16,8]{0,1:T(8,128)S(1)}, f32[16,8]{0,1:T(8,128)}, u32[]{:S(2)}) copy-start(f32[16,8]{0,1:T(8,128)} %param.8) | copy-start | bytes 1540

commit v8 on v7

--- a/solution.py
+++ b/solution.py
@@ -52,12 +52,12 @@
     wide = tok_parts.shape[1]
     experts = out_ref.shape[0] // ROWS
     ids_load = pltpu.make_async_copy(ids_hbm, ids_ref, sems.at[PARTS])
-    ids_load.start()
+    ids_load.start(priority=1)
     loads = []
     for part in range(PARTS):
         source = tok_hbm.at[:, pl.ds(part * wide, wide)]
         loads.append(pltpu.make_async_copy(source, tok_parts.at[pl.ds(part * toks, toks), :], sems.at[part]))
-        loads[-1].start()
+        loads[-1].start(priority=1)
     ids_load.wait()
     filled = routing(ids_ref[...], experts)
     filled_ref[...] = filled.astype(BF16)

time: 87.5 us -> 87.5 us (level)
  no operation moved by 1% of the time
where the time goes in v8:
time: 87.5 us; the launch traced here: 87.3 us
  blocking collectives  76.1 us (87%)
  Pallas kernels  11.1 us (13%)
    all_to_all x2, blocking collectives, exchange(): lax.all_to_all(rows.reshape(experts, ROWS, wide), ('node', 'local'), spli...  76.1 us
    pallas_call x1, Pallas kernels, on_device(): pl.pallas_call(expert_kernel, out_shape=[slots, jax.ShapeDtypeStruct((3 *...  7.86 us
    pallas_call x1, Pallas kernels, on_device(): pl.pallas_call(dispatch_kernel, out_shape=[slots, jax.ShapeDtypeStruct((t...  2.02 us

profile of v8, /device:TPU:1, one launch (start us, length us, event | category | flops | bytes accessed | tf_op | source)
XLA Modules:
  0.0 87.3 jit_solution(966257837221139923)
XLA Ops:
  0.0 0.0 slice-start
  0.0 0.0 slice-start.2
  0.0 0.0 slice-start.4
  0.0 0.0 slice-start.1
  0.0 0.0 slice-start.3
  0.0 0.0 slice-start.5
  0.0 2.0 %dispatch.1 = (bf16[1024,1024]{1,0:T(8,128)(2,1)S(1)}, bf16[16,1024]{1,0:T(8,128)(2,1)S(1)}) custom-call(s32[8,16]{1,0:T(8,128)} %bitcast.22, bf16[16,4096]{1,0:T(8,128)(2,1)} %tok_hbm.1), custom_call_target="tpu_custom_call" | custom-call | flops 20000000000 | bytes 100000000 | tf_op jit(solution)/shard_map/dispatch/pallas_call | solution.py:164
  2.1 0.0 copy-start
  2.1 0.0 copy-start.1
  2.1 41.9 %all_to_all.10 = bf16[128,8,1024]{2,1,0:T(8,128)(2,1)S(1)} all-to-all(bf16[128,8,1024]{2,1,0:T(8,128)(2,1)S(1)} %bitcast.21), channel_id=1, replica_groups=mesh['node'=32,'local'=4] {'node','local'}, dimensions={0} | all-to-all | bytes 4194304 | tf_op jit(solution)/shard_map/all_to_all | solution.py:159
  44.0 0.0 slice-done
  44.0 0.0 slice-done.2
  44.0 0.0 slice-done.4
  44.0 0.0 slice-done.1
  44.0 0.0 slice-done.3
  44.0 0.0 slice-done.5
  44.0 0.0 copy-done
  44.0 0.0 copy-done.1
  44.0 7.9 %expert.1 = (bf16[1024,1024]{1,0:T(8,128)(2,1)S(1)}, bf16[192,1024]{1,0:T(8,128)(2,1)S(1)}) custom-call(s32[8,16]{1,0:T(8,128)S(1)} %bitcast.23, f32[8,16]{1,0:T(8,128)S(1)} %bitcast.24, bf16[16,1024]{1,0:T(8,128)(2,1)S(1)} %get-tuple-element.9.filled_ref, bf16[1024,1024]{1,0:T(8,128)(2,1)S(1)} %bitcast.18, bf16[4096,1024]{1,0:T(8,128)(2,1)S(1)} %bitcast.11, ...), custom_call_target="tpu_custom_call" | custom-call | flops 6499999744 | bytes 30000000 | tf_op jit(solution)/shard_map/expert/pallas_call | solution.py:178
  51.9 34.2 %all_to_all.11 = bf16[128,8,1024]{2,1,0:T(8,128)(2,1)S(1)} all-to-all(bf16[128,8,1024]{2,1,0:T(8,128)(2,1)S(1)} %bitcast.20), channel_id=1, replica_groups=mesh['node'=32,'local'=4] {'node','local'}, dimensions={0} | all-to-all | bytes 4194304 | tf_op jit(solution)/shard_map/all_to_all | solution.py:159
  86.1 1.2 %combine.1 = bf16[16,4096]{1,0:T(8,128)(2,1)} custom-call(bf16[192,1024]{1,0:T(8,128)(2,1)S(1)} %get-tuple-element.11.weights_ref, bf16[1024,1024]{1,0:T(8,128)(2,1)S(1)} %bitcast.19), custom_call_target="tpu_custom_call" | custom-call | tf_op jit(solution)/shard_map/combine/pallas_call | solution.py:191
  (3 shorter events, 0.0 us)
Async XLA Ops:
  0.0 44.0 %slice-start = ((s8[8388608]{0:T(1024)(128)(4,1)}), s8[4194304]{0:T(1024)(128)(4,1)S(1)}, s32[]{:S(2)}) async-start(s8[8388608]{0:T(1024)(128)(4,1)} %bitcast.9), calls=%async_computation.2 | async-start | bytes 8388608
  0.0 44.0 %slice-start.2 = ((s8[8388608]{0:T(1024)(128)(4,1)}), s8[4194304]{0:T(1024)(128)(4,1)S(1)}, s32[]{:S(2)}) async-start(s8[8388608]{0:T(1024)(128)(4,1)} %bitcast.12), calls=%async_computation.4 | async-start | bytes 8388608
  0.0 44.0 %slice-start.4 = ((s8[8388608]{0:T(1024)(128)(4,1)}), s8[4194304]{0:T(1024)(128)(4,1)S(1)}, s32[]{:S(2)}) async-start(s8[8388608]{0:T(1024)(128)(4,1)} %bitcast.15), calls=%async_computation.6 | async-start | bytes 8388608
  0.0 44.0 %slice-start.1 = ((s8[8388608]{0:T(1024)(128)(4,1)}), s8[4194304]{0:T(1024)(128)(4,1)S(1)}, s32[]{:S(2)}) async-start(s8[8388608]{0:T(1024)(128)(4,1)} %bitcast.9), calls=%async_computation.3 | async-start | bytes 8388608
  0.0 44.0 %slice-start.3 = ((s8[8388608]{0:T(1024)(128)(4,1)}), s8[4194304]{0:T(1024)(128)(4,1)S(1)}, s32[]{:S(2)}) async-start(s8[8388608]{0:T(1024)(128)(4,1)} %bitcast.12), calls=%async_computation.5 | async-start | bytes 8388608
  0.0 44.0 %slice-start.5 = ((s8[8388608]{0:T(1024)(128)(4,1)}), s8[4194304]{0:T(1024)(128)(4,1)S(1)}, s32[]{:S(2)}) async-start(s8[8388608]{0:T(1024)(128)(4,1)} %bitcast.15), calls=%async_computation.7 | async-start | bytes 8388608
  2.1 41.9 %copy-start = (s32[16,8]{0,1:T(8,128)S(1)}, s32[16,8]{0,1:T(8,128)}, u32[]{:S(2)}) copy-start(s32[16,8]{0,1:T(8,128)} %param.7) | copy-start | bytes 1540
  2.1 41.9 %copy-start.1 = (f32[16,8]{0,1:T(8,128)S(1)}, f32[16,8]{0,1:T(8,128)}, u32[]{:S(2)}) copy-start(f32[16,8]{0,1:T(8,128)} %param.8) | copy-start | bytes 1540
